TPU v7x, 32 devices: a whole 2x2x4 slice. The times are simulated.
32 devices in a mesh: ctx: 4 (over x, core), wsh: 8 (over z, y).
Axes of the slice: x: 2, y: 2, z: 4, core: 2. Of those that a mesh axis runs over, the one named last changes fastest.
Arguments:
- layer_input: bfloat16 [8, 1024, 768], P('wsh', 'ctx'), may hold values from -6 to 6
- encoder_states: bfloat16 [8, 512, 768], P('wsh', 'ctx'), may hold values from -6 to 6
- block_order: int32 [8, 8], P('wsh'), may hold values from 0 to 7, each once within a row
- out_grad: bfloat16 [8, 1024, 768], P('wsh', 'ctx'), may hold values from -6 to 6
- self_gain: bfloat16 [768], P('wsh'), may hold values from 0.5 to 1.5
- query_self: bfloat16 [768, 768], P('wsh'), may hold values from -0.109375 to 0.109375
- key_self: bfloat16 [768, 768], P('wsh'), may hold values from -0.109375 to 0.109375
- value_self: bfloat16 [768, 768], P('wsh'), may hold values from -0.21875 to 0.21875
- output_self: bfloat16 [768, 768], P('wsh'), may hold values from -0.875 to 0.875
- bias_table: bfloat16 [32, 12], P('wsh'), may hold values from -4 to 4
- cross_gain: bfloat16 [768], P('wsh'), may hold values from 0.5 to 1.5
- cross_query_weight: bfloat16 [768, 768], P('wsh'), may hold values from -0.109375 to 0.109375
- key_cross: bfloat16 [768, 768], P('wsh'), may hold values from -0.109375 to 0.109375
- value_cross: bfloat16 [768, 768], P('wsh'), may hold values from -0.21875 to 0.21875
- output_cross: bfloat16 [768, 768], P('wsh'), may hold values from -0.875 to 0.875
- ffn_gain: bfloat16 [768], P('wsh'), may hold values from 0.5 to 1.5
- ffn_gate: bfloat16 [768, 2048], P('wsh'), may hold values from -0.21875 to 0.21875
- ffn_up: bfloat16 [768, 2048], P('wsh'), may hold values from -0.21875 to 0.21875
- ffn_down: bfloat16 [2048, 768], P('wsh'), may hold values from -0.125 to 0.125
Outputs:
- layer_output: bfloat16 [8, 1024, 768], P('wsh', 'ctx')
- input_grad: float32 [8, 1024, 768], P('wsh', 'ctx')
- encoder_state_gradient: float32 [8, 512, 768], P('wsh', 'ctx')
- self_gain_grad: float32 [768], P('wsh')
- query_self_grad: float32 [768, 768], P('wsh')
- key_self_grad: float32 [768, 768], P('wsh')
- value_self_grad: float32 [768, 768], P('wsh')
- output_self_grad: float32 [768, 768], P('wsh')
- bias_table_grad: float32 [32, 12], P('wsh')
- cross_gain_grad: float32 [768], P('wsh')
- query_cross_grad: float32 [768, 768], P('wsh')
- key_cross_grad: float32 [768, 768], P('wsh')
- value_cross_grad: float32 [768, 768], P('wsh')
- output_cross_grad: float32 [768, 768], P('wsh')
- ffn_gain_grad: float32 [768], P('wsh')
- ffn_gate_grad: float32 [768, 2048], P('wsh')
- ffn_up_grad: float32 [768, 2048], P('wsh')
- ffn_down_grad: float32 [2048, 768], P('wsh')
Inputs may be any that keep to these rules, and one draw needn't show every extreme that they name: Each row is a permutation: stored block j of sequence s holds the positions block_order[s, j] * 128 to block_order[s, j] * 128 + 127 of that sequence.
All inputs are finite; a program needn't handle non-finite values.
Results may differ from a plain program's by a relative error of at most 0.03.
Values may be sent and summed in bfloat16 or wider, within the bound.
A program may use at most 192 MiB of HBM per device.

v0:
```python
import math

import jax
import jax.numpy as jnp
from jax import lax
from jax.sharding import PartitionSpec as P

norm_eps = 1e-06
neg_big = -1000000000.0


def bucket_index(distance):
    counter = jnp.zeros_like(distance)
    for number in range(1, 16):
        threshold = math.ceil(16 * 8 ** (number / 16))
        counter = counter + (distance >= threshold).astype(distance.dtype)
    return jnp.where(distance < 16, distance, 16 + counter)


def gelu_tanh(values):
    return jax.nn.gelu(values, approximate=True)


def rms_forward(values, gain_vec):
    inv_rms = lax.rsqrt(jnp.mean(values * values, axis=-1, keepdims=True) + norm_eps)
    return (values * inv_rms * gain_vec, inv_rms)


def rms_backward(values, inv_rms, gain_vec, normalized_grad):
    weighted = normalized_grad * gain_vec
    gain_grad = jnp.sum(normalized_grad * values * inv_rms, axis=0)
    inner_mean = jnp.mean(weighted * values, axis=-1, keepdims=True)
    return (inv_rms * weighted - values * (inv_rms * inv_rms * inv_rms) * inner_mean, gain_grad)


def matmul(left_side, right_side):
    return jnp.dot(left_side, right_side, preferred_element_type=jnp.float32)


def matmul_tn(left_side, right_side):
    return lax.dot_general(
        left_side, right_side, (((0,), (0,)), ((), ())), preferred_element_type=jnp.float32
    )


def matmul_nt(left_side, right_side):
    return lax.dot_general(
        left_side, right_side, (((1,), (1,)), ((), ())), preferred_element_type=jnp.float32
    )


def split_heads(matrix, head_count):
    return jnp.transpose(matrix.reshape(matrix.shape[0], head_count, -1), (1, 0, 2))


def join_heads(tensor):
    return jnp.transpose(tensor, (1, 0, 2)).reshape(tensor.shape[1], -1)


def bucket_onehot(query_pos, key_pos, bucket_count):
    distance = query_pos[:, None] - key_pos[None, :]
    buckets = bucket_index(jnp.maximum(distance, 0))
    selection_flag = (
        buckets[None] == jnp.arange(bucket_count, dtype=buckets.dtype)[:, None, None]
    ).astype(jnp.bfloat16)
    return (selection_flag, distance >= 0)


def self_bias_maker(query_pos, entire_position_bias_table, bucket_count):

    def maker(key_pos):
        selection_flag, allowed = bucket_onehot(query_pos, key_pos, bucket_count)
        bias_tile = jnp.einsum(
            "dvc,dz->zvc",
            selection_flag,
            entire_position_bias_table,
            preferred_element_type=jnp.float32,
        )
        return (bias_tile, allowed, selection_flag)

    return maker


def masked_bias_tiles(query_pos, key_marks, entire_position_bias_table, bucket_count):
    maker = self_bias_maker(query_pos, entire_position_bias_table, bucket_count)

    def one_tile(key_pos):
        bias_tile, allowed, unused = maker(key_pos)
        return jnp.where(allowed[None], bias_tile, neg_big).astype(jnp.bfloat16)

    return lax.map(one_tile, key_marks)


def score_tile(query_heads, key_tile, bias_tile):
    scores = jnp.einsum("hqd,khd->hqk", query_heads, key_tile, preferred_element_type=jnp.float32)
    if bias_tile is None:
        return scores
    return scores + bias_tile.astype(jnp.float32)


def attend_forward(query_heads, key_tiles, value_tiles, bias_tiles):
    row_shape = (query_heads.shape[0], query_heads.shape[1])

    def measure(carry, slices):
        row_max, row_total = carry
        scores = score_tile(query_heads, slices[0], slices[1])
        new_max = jnp.maximum(row_max, jnp.max(scores, axis=-1))
        row_total = row_total * jnp.exp(row_max - new_max) + jnp.sum(
            jnp.exp(scores - new_max[..., None]), axis=-1
        )
        return ((new_max, row_total), None)

    initial = (jnp.full(row_shape, neg_big, jnp.float32), jnp.zeros(row_shape, jnp.float32))
    (row_max, row_total), unused = lax.scan(measure, initial, (key_tiles, bias_tiles))
    log_total = row_max + jnp.log(row_total)

    def collect(running, slices):
        scores = score_tile(query_heads, slices[0], slices[2])
        weights = jnp.exp(scores - log_total[..., None]).astype(jnp.bfloat16)
        return (
            running
            + jnp.einsum("hqk,khd->hqd", weights, slices[1], preferred_element_type=jnp.float32),
            None,
        )

    blended, unused = lax.scan(
        collect, jnp.zeros(query_heads.shape, jnp.float32), (key_tiles, value_tiles, bias_tiles)
    )
    return (blended, log_total)


def attend_backward(
    query_heads,
    key_tiles,
    value_tiles,
    bias_tiles,
    key_marks,
    query_pos,
    log_total,
    output_grad,
    blended,
    bucket_count,
):
    delta_rows = jnp.sum(output_grad.astype(jnp.float32) * blended, axis=-1)

    def sweep(carry, slices):
        query_grad, table_grad = carry
        key_tile, value_tile, bias_tile, marks = slices
        scores = score_tile(query_heads, key_tile, bias_tile)
        probs = jnp.exp(scores - log_total[..., None])
        probs_grad = jnp.einsum(
            "hqd,khd->hqk", output_grad, value_tile, preferred_element_type=jnp.float32
        )
        gradient_of_scores = (probs * (probs_grad - delta_rows[..., None])).astype(jnp.bfloat16)
        query_grad = query_grad + jnp.einsum(
            "hqk,khd->hqd", gradient_of_scores, key_tile, preferred_element_type=jnp.float32
        )
        if bias_tile is not None:
            selection_flag, unused = bucket_onehot(query_pos, marks, bucket_count)
            table_grad = table_grad + jnp.einsum(
                "exo,dxo->ed",
                selection_flag,
                gradient_of_scores,
                preferred_element_type=jnp.float32,
            )
        key_grad = jnp.einsum(
            "hqk,hqd->khd", gradient_of_scores, query_heads, preferred_element_type=jnp.float32
        )
        value_grad = jnp.einsum(
            "hqk,hqd->khd",
            probs.astype(jnp.bfloat16),
            output_grad,
            preferred_element_type=jnp.float32,
        )
        return ((query_grad, table_grad), (key_grad, value_grad))

    initial = (
        jnp.zeros(query_heads.shape, jnp.float32),
        jnp.zeros((bucket_count, query_heads.shape[0]), jnp.float32),
    )
    (query_grad, table_grad), key_side = lax.scan(
        sweep, initial, (key_tiles, value_tiles, bias_tiles, key_marks)
    )
    key_grads, value_grads = key_side
    key_total = key_grads.shape[0] * key_grads.shape[1]
    return (
        query_grad,
        key_grads.reshape(key_total, -1),
        value_grads.reshape(key_total, -1),
        table_grad,
        delta_rows,
    )


def on_device(
    layer_input,
    encoder_states,
    block_order,
    out_grad,
    self_gain,
    query_self,
    key_self,
    value_self,
    output_self,
    bias_table,
    cross_gain,
    cross_query_weight,
    key_cross,
    value_cross,
    output_cross,
    ffn_gain,
    ffn_gate,
    ffn_up,
    ffn_down,
):
    head_count = bias_table.shape[1]
    bucket_count = bias_table.shape[0] * lax.axis_size("wsh")
    row_count = layer_input.shape[1]
    seq_total = row_count * lax.axis_size("ctx")
    block_rows = seq_total // block_order.shape[1]
    key_block = math.gcd(seq_total, 512)
    enc_total = encoder_states.shape[1] * lax.axis_size("ctx")
    encoder_block_rows = math.gcd(enc_total, 512)
    self_set = (
        lax.all_gather(self_gain, "wsh", axis=0, tiled=True),
        lax.all_gather(query_self, "wsh", axis=0, tiled=True),
        lax.all_gather(key_self, "wsh", axis=0, tiled=True),
        lax.all_gather(value_self, "wsh", axis=0, tiled=True),
        lax.all_gather(output_self, "wsh", axis=0, tiled=True),
        lax.all_gather(bias_table, "wsh", axis=0, tiled=True),
    )
    cross_set = (
        lax.all_gather(cross_gain, "wsh", axis=0, tiled=True),
        lax.all_gather(cross_query_weight, "wsh", axis=0, tiled=True),
        lax.all_gather(key_cross, "wsh", axis=0, tiled=True),
        lax.all_gather(value_cross, "wsh", axis=0, tiled=True),
        lax.all_gather(output_cross, "wsh", axis=0, tiled=True),
    )
    ffn_set = (
        lax.all_gather(ffn_gain, "wsh", axis=0, tiled=True),
        lax.all_gather(ffn_gate, "wsh", axis=0, tiled=True),
        lax.all_gather(ffn_up, "wsh", axis=0, tiled=True),
        lax.all_gather(ffn_down, "wsh", axis=0, tiled=True),
    )
    ctx_index = lax.axis_index("ctx")
    order_row = block_order[0]
    key_pos = (
        order_row[:, None] * block_rows + jnp.arange(block_rows, dtype=jnp.int32)[None, :]
    ).reshape(-1)
    query_pos = lax.dynamic_slice_in_dim(key_pos, ctx_index * row_count, row_count)
    self_marks = key_pos.reshape(-1, key_block)
    inputs_now = layer_input[0].astype(jnp.float32)
    normed_one, inv_one = rms_forward(inputs_now, self_set[0].astype(jnp.float32))
    normed_one = normed_one.astype(jnp.bfloat16)
    queries_one = matmul(normed_one, self_set[1]).astype(jnp.bfloat16)
    keys_one = matmul(normed_one, self_set[2]).astype(jnp.bfloat16)
    values_one = matmul(normed_one, self_set[3]).astype(jnp.bfloat16)
    encoder_rows = encoder_states[0]
    keys_enc = matmul(encoder_rows, cross_set[2]).astype(jnp.bfloat16)
    values_enc = matmul(encoder_rows, cross_set[3]).astype(jnp.bfloat16)
    keys_all, value_rows_total, keys_far, values_far = (
        lax.all_gather(keys_one, "ctx", axis=0, tiled=True),
        lax.all_gather(values_one, "ctx", axis=0, tiled=True),
        lax.all_gather(keys_enc, "ctx", axis=0, tiled=True),
        lax.all_gather(values_enc, "ctx", axis=0, tiled=True),
    )
    model_width = keys_all.shape[1]
    head_size = model_width // head_count
    keys_self_attention = keys_all.reshape(-1, key_block, head_count, head_size)
    self_values = value_rows_total.reshape(-1, key_block, head_count, head_size)
    cross_keys = keys_far.reshape(-1, encoder_block_rows, head_count, head_size)
    cross_values = values_far.reshape(-1, encoder_block_rows, head_count, head_size)
    heads_one = split_heads(queries_one, head_count)
    self_bias = masked_bias_tiles(query_pos, self_marks, self_set[5], bucket_count)
    blended_one, log_one = attend_forward(heads_one, keys_self_attention, self_values, self_bias)
    attn_self = join_heads(blended_one).astype(jnp.bfloat16)
    section_two = inputs_now + matmul(attn_self, self_set[4])
    normed_two, inv_two = rms_forward(section_two, cross_set[0].astype(jnp.float32))
    normed_two = normed_two.astype(jnp.bfloat16)
    queries_two = matmul(normed_two, cross_set[1]).astype(jnp.bfloat16)
    heads_two = split_heads(queries_two, head_count)
    blended_two, log_two = attend_forward(heads_two, cross_keys, cross_values, None)
    attn_cross = join_heads(blended_two).astype(jnp.bfloat16)
    section_three = section_two + matmul(attn_cross, cross_set[4])
    normed_three, inv_three = rms_forward(section_three, ffn_set[0].astype(jnp.float32))
    normed_three = normed_three.astype(jnp.bfloat16)
    gate_pre = matmul(normed_three, ffn_set[1])
    up_pre = matmul(normed_three, ffn_set[2])
    activated, gelu_pull = jax.vjp(gelu_tanh, gate_pre)
    hidden = (activated * up_pre).astype(jnp.bfloat16)
    result = (section_three + matmul(hidden, ffn_set[3])).astype(jnp.bfloat16)
    ffn_back = (
        lax.all_gather(ffn_gain, "wsh", axis=0, tiled=True),
        lax.all_gather(ffn_gate, "wsh", axis=0, tiled=True),
        lax.all_gather(ffn_up, "wsh", axis=0, tiled=True),
        lax.all_gather(ffn_down, "wsh", axis=0, tiled=True),
    )
    grad_now = out_grad[0].astype(jnp.float32)
    grad_three = grad_now.astype(jnp.bfloat16)
    down_part = matmul_tn(hidden, grad_three)
    hidden_grad = matmul_nt(grad_three, ffn_back[3])
    gate_grad = gelu_pull(hidden_grad * up_pre)[0].astype(jnp.bfloat16)
    up_grad = (hidden_grad * activated).astype(jnp.bfloat16)
    gate_part = matmul_tn(normed_three, gate_grad)
    up_part = matmul_tn(normed_three, up_grad)
    normed_three_grad = matmul_nt(gate_grad, ffn_back[1]) + matmul_nt(up_grad, ffn_back[2])
    extra_three, ffn_gain_part = rms_backward(
        section_three, inv_three, ffn_back[0].astype(jnp.float32), normed_three_grad
    )
    section_three_grad = grad_now + extra_three
    ffn_parts = (
        lax.psum_scatter(
            ffn_gain_part.astype(jnp.bfloat16), "wsh", scatter_dimension=0, tiled=True
        ).astype(jnp.float32),
        lax.psum_scatter(
            gate_part.astype(jnp.bfloat16), "wsh", scatter_dimension=0, tiled=True
        ).astype(jnp.float32),
        lax.psum_scatter(
            up_part.astype(jnp.bfloat16), "wsh", scatter_dimension=0, tiled=True
        ).astype(jnp.float32),
        lax.psum_scatter(
            down_part.astype(jnp.bfloat16), "wsh", scatter_dimension=0, tiled=True
        ).astype(jnp.float32),
    )
    cross_back = (
        lax.all_gather(cross_gain, "wsh", axis=0, tiled=True),
        lax.all_gather(cross_query_weight, "wsh", axis=0, tiled=True),
        lax.all_gather(key_cross, "wsh", axis=0, tiled=True),
        lax.all_gather(value_cross, "wsh", axis=0, tiled=True),
        lax.all_gather(output_cross, "wsh", axis=0, tiled=True),
    )
    branch_two_grad = section_three_grad.astype(jnp.bfloat16)
    output_cross_part = matmul_tn(attn_cross, branch_two_grad)
    attn_cross_grad = matmul_nt(branch_two_grad, cross_back[4]).astype(jnp.bfloat16)
    query_two_grad, far_key_grad, far_value_grad, unused, unused_delta = attend_backward(
        heads_two,
        cross_keys,
        cross_values,
        None,
        None,
        query_pos,
        log_two,
        split_heads(attn_cross_grad, head_count),
        blended_two,
        1,
    )
    distant_key_portion, far_value_share = (
        lax.psum_scatter(
            far_key_grad.astype(jnp.bfloat16), "ctx", scatter_dimension=0, tiled=True
        ).astype(jnp.float32),
        lax.psum_scatter(
            far_value_grad.astype(jnp.bfloat16), "ctx", scatter_dimension=0, tiled=True
        ).astype(jnp.float32),
    )
    far_key_low = distant_key_portion.astype(jnp.bfloat16)
    far_value_low = far_value_share.astype(jnp.bfloat16)
    key_cross_part = matmul_tn(encoder_rows, far_key_low)
    value_cross_part = matmul_tn(encoder_rows, far_value_low)
    encoder_state_gradient = matmul_nt(far_key_low, cross_back[2]) + matmul_nt(
        far_value_low, cross_back[3]
    )
    query_two_low = join_heads(query_two_grad).astype(jnp.bfloat16)
    query_cross_part = matmul_tn(normed_two, query_two_low)
    normed_two_grad = matmul_nt(query_two_low, cross_back[1])
    extra_two, cross_gain_part = rms_backward(
        section_two, inv_two, cross_back[0].astype(jnp.float32), normed_two_grad
    )
    section_two_grad = section_three_grad + extra_two
    cross_parts = (
        lax.psum_scatter(
            cross_gain_part.astype(jnp.bfloat16), "wsh", scatter_dimension=0, tiled=True
        ).astype(jnp.float32),
        lax.psum_scatter(
            query_cross_part.astype(jnp.bfloat16), "wsh", scatter_dimension=0, tiled=True
        ).astype(jnp.float32),
        lax.psum_scatter(
            key_cross_part.astype(jnp.bfloat16), "wsh", scatter_dimension=0, tiled=True
        ).astype(jnp.float32),
        lax.psum_scatter(
            value_cross_part.astype(jnp.bfloat16), "wsh", scatter_dimension=0, tiled=True
        ).astype(jnp.float32),
        lax.psum_scatter(
            output_cross_part.astype(jnp.bfloat16), "wsh", scatter_dimension=0, tiled=True
        ).astype(jnp.float32),
    )
    self_back = (
        lax.all_gather(self_gain, "wsh", axis=0, tiled=True),
        lax.all_gather(query_self, "wsh", axis=0, tiled=True),
        lax.all_gather(key_self, "wsh", axis=0, tiled=True),
        lax.all_gather(value_self, "wsh", axis=0, tiled=True),
        lax.all_gather(output_self, "wsh", axis=0, tiled=True),
        lax.all_gather(bias_table, "wsh", axis=0, tiled=True),
    )
    branch_one_grad = section_two_grad.astype(jnp.bfloat16)
    output_self_part = matmul_tn(attn_self, branch_one_grad)
    attn_self_grad = matmul_nt(branch_one_grad, self_back[4]).astype(jnp.bfloat16)
    query_one_grad, own_key_grad, own_value_grad, table_part, delta_one = attend_backward(
        heads_one,
        keys_self_attention,
        self_values,
        self_bias,
        self_marks,
        query_pos,
        log_one,
        split_heads(attn_self_grad, head_count),
        blended_one,
        bucket_count,
    )
    local_key_portion, own_value_share = (
        lax.psum_scatter(
            own_key_grad.astype(jnp.bfloat16), "ctx", scatter_dimension=0, tiled=True
        ).astype(jnp.float32),
        lax.psum_scatter(
            own_value_grad.astype(jnp.bfloat16), "ctx", scatter_dimension=0, tiled=True
        ).astype(jnp.float32),
    )
    own_key_low = local_key_portion.astype(jnp.bfloat16)
    own_value_low = own_value_share.astype(jnp.bfloat16)
    query_one_low = join_heads(query_one_grad).astype(jnp.bfloat16)
    query_self_part = matmul_tn(normed_one, query_one_low)
    key_self_part = matmul_tn(normed_one, own_key_low)
    value_self_part = matmul_tn(normed_one, own_value_low)
    normed_one_grad = (
        matmul_nt(query_one_low, self_back[1])
        + matmul_nt(own_key_low, self_back[2])
        + matmul_nt(own_value_low, self_back[3])
    )
    additional_first, self_gain_portion = rms_backward(
        inputs_now, inv_one, self_back[0].astype(jnp.float32), normed_one_grad
    )
    input_grad = section_two_grad + additional_first
    self_parts = (
        lax.psum_scatter(
            self_gain_portion.astype(jnp.bfloat16), "wsh", scatter_dimension=0, tiled=True
        ).astype(jnp.float32),
        lax.psum_scatter(
            query_self_part.astype(jnp.bfloat16), "wsh", scatter_dimension=0, tiled=True
        ).astype(jnp.float32),
        lax.psum_scatter(
            key_self_part.astype(jnp.bfloat16), "wsh", scatter_dimension=0, tiled=True
        ).astype(jnp.float32),
        lax.psum_scatter(
            value_self_part.astype(jnp.bfloat16), "wsh", scatter_dimension=0, tiled=True
        ).astype(jnp.float32),
        lax.psum_scatter(
            output_self_part.astype(jnp.bfloat16), "wsh", scatter_dimension=0, tiled=True
        ).astype(jnp.float32),
        lax.psum_scatter(
            table_part.astype(jnp.bfloat16), "wsh", scatter_dimension=0, tiled=True
        ).astype(jnp.float32),
    )
    summed = (
        lax.psum(self_parts[0].astype(jnp.bfloat16), "ctx").astype(jnp.float32),
        lax.psum(self_parts[1].astype(jnp.bfloat16), "ctx").astype(jnp.float32),
        lax.psum(self_parts[2].astype(jnp.bfloat16), "ctx").astype(jnp.float32),
        lax.psum(self_parts[3].astype(jnp.bfloat16), "ctx").astype(jnp.float32),
        lax.psum(self_parts[4].astype(jnp.bfloat16), "ctx").astype(jnp.float32),
        lax.psum(self_parts[5].astype(jnp.bfloat16), "ctx").astype(jnp.float32),
        lax.psum(cross_parts[0].astype(jnp.bfloat16), "ctx").astype(jnp.float32),
        lax.psum(cross_parts[1].astype(jnp.bfloat16), "ctx").astype(jnp.float32),
        lax.psum(cross_parts[2].astype(jnp.bfloat16), "ctx").astype(jnp.float32),
        lax.psum(cross_parts[3].astype(jnp.bfloat16), "ctx").astype(jnp.float32),
        lax.psum(cross_parts[4].astype(jnp.bfloat16), "ctx").astype(jnp.float32),
        lax.psum(ffn_parts[0].astype(jnp.bfloat16), "ctx").astype(jnp.float32),
        lax.psum(ffn_parts[1].astype(jnp.bfloat16), "ctx").astype(jnp.float32),
        lax.psum(ffn_parts[2].astype(jnp.bfloat16), "ctx").astype(jnp.float32),
        lax.psum(ffn_parts[3].astype(jnp.bfloat16), "ctx").astype(jnp.float32),
    )
    return (
        result[None],
        input_grad[None],
        encoder_state_gradient[None],
        summed[0],
        summed[1],
        summed[2],
        summed[3],
        summed[4],
        summed[5],
        summed[6],
        summed[7],
        summed[8],
        summed[9],
        summed[10],
        summed[11],
        summed[12],
        summed[13],
        summed[14],
    )


def solution(mesh):
    in_specs = (
        P("wsh", "ctx", None),
        P("wsh", "ctx", None),
        P("wsh", None),
        P("wsh", "ctx", None),
        P("wsh"),
        P("wsh", None),
        P("wsh", None),
        P("wsh", None),
        P("wsh", None),
        P("wsh", None),
        P("wsh"),
        P("wsh", None),
        P("wsh", None),
        P("wsh", None),
        P("wsh", None),
        P("wsh"),
        P("wsh", None),
        P("wsh", None),
        P("wsh", None),
    )
    out_specs = (
        P("wsh", "ctx", None),
        P("wsh", "ctx", None),
        P("wsh", "ctx", None),
        P("wsh"),
        P("wsh", None),
        P("wsh", None),
        P("wsh", None),
        P("wsh", None),
        P("wsh", None),
        P("wsh"),
        P("wsh", None),
        P("wsh", None),
        P("wsh", None),
        P("wsh", None),
        P("wsh"),
        P("wsh", None),
        P("wsh", None),
        P("wsh", None),
    )
    return jax.shard_map(
        on_device, mesh=mesh, in_specs=in_specs, out_specs=out_specs, check_vma=False
    )
```

profile of v0, /device:TPU:0, one launch (start us, length us, event | category | flops | bytes accessed | tf_op | source)
XLA Modules:
  0.0 1562.7 jit_solution(17012285406103362583)
XLA Ops:
  15.2 23.4 %all-reduce.8 = (bf16[768]{0:T(1024)(128)(2,1)S(1)}, bf16[768]{0:T(1024)(128)(2,1)S(1)}, bf16[768]{0:T(1024)(128)(2,1)S(1)}) all-reduce(bf16[768]{0:T(1024)(128)(2,1)S(1)} %dynamic-update-slice, bf16[768]{0:T(1024)(128)(2,1)S(1)} %dynamic-update-slice.1, bf16[768]{0:T(1024)(128)(2,1)S(1)} %dynamic-update-slice.2), channel_id=1, replica_groups=mesh['ctx'=4,'wsh'=8] {'wsh'}, use_global_device_ids=true, to_apply=%add | all-reduce | flops 2304 | bytes 9216
  40.3 13.7 all-gather.15.cloned.1.call-done
  56.8 39.3 %all-gather.21.cloned.1.call-done = bf16[768,768]{1,0:T(8,128)(2,1)} async-done(((bf16[96,768]{1,0:T(8,128)(2,1)}), bf16[768,768]{1,0:T(8,128)(2,1)}) %all-gather.21.cloned.1.call-update) | async-done | bytes 1179664 | tf_op jit(solution)/shard_map/all_gather | solution.py:228
  103.2 18.4 %all-gather = bf16[8,4,12]{2,1,0:T(4,128)(2,1)S(1)} all-gather(bf16[1,4,12]{2,1,0:T(4,128)(2,1)S(1)} %bitcast.383), channel_id=1, replica_groups=mesh['ctx'=4,'wsh'=8] {'wsh'}, dimensions={0}, use_global_device_ids=true | all-gather | bytes 864 | tf_op jit(solution)/shard_map/all_gather | solution.py:230
  121.8 28.6 %while.16 = (s32[]{:T(128)}, bf16[2,12,256,512]{2,3,1,0:T(8,128)(2,1)}, s32[256]{0:T(256)S(1)}, s32[2,512]{1,0:T(2,128)S(1)}, bf16[32,12]{0,1:T(8,128)(2,1)S(1)}, /*index=5*/s32[]{:T(128)}) while((s32[]{:T(128)}, bf16[2,12,256,512]{2,3,1,0:T(8,128)(2,1)}, s32[256]{0:T(256)S(1)}, s32[2,512]{1,0:T(2,128)S(1)}, bf16[32,12]{0,1:T(8,128)(2,1)S(1)}, ...), condition=%wide.region_2.3_spmd, body=%wide.region_1.2_spmd.sunk | while | flops 114688000 | bytes 17050952 | solution.py:91
  122.9 5.0 fusion.244
  127.9 6.2 copy.168
  137.1 5.0 fusion.244
  142.1 6.2 copy.168
  152.5 27.7 %all-gather.29.cloned.1.call-done = bf16[768,768]{1,0:T(8,128)(2,1)} async-done(((bf16[96,768]{1,0:T(8,128)(2,1)}), bf16[768,768]{1,0:T(8,128)(2,1)}) %all-gather.29.cloned.1.call-update) | async-done | bytes 1179664 | tf_op jit(solution)/shard_map/all_gather | solution.py:235
  181.7 8.6 all_gather.82
  191.5 30.6 %all-gather.31.cloned.1.call-done = bf16[768,768]{1,0:T(8,128)(2,1)} async-done(((bf16[96,768]{1,0:T(8,128)(2,1)}), bf16[768,768]{1,0:T(8,128)(2,1)}) %all-gather.31.cloned.1.call-update) | async-done | bytes 1179664 | tf_op jit(solution)/shard_map/all_gather | solution.py:236
  223.6 8.6 all_gather.84
  233.4 9.1 all-gather.17.cloned.1.call-done
  248.5 21.3 %while.17 = (s32[]{:T(128)}, f32[12,256]{1,0:T(8,128)S(1)}, f32[12,256]{1,0:T(8,128)S(1)}, bf16[2,512,12,64]{1,3,2,0:T(8,128)(2,1)S(1)}, bf16[12,256,64]{1,2,0:T...) while((s32[]{:T(128)}, f32[12,256]{1,0:T(8,128)S(1)}, ...), condition=%wide.region_6.7_spmd.clone, body=%wide.region_3.6_spmd.clone.sunk | while | flops 212352000 | bytes 20214884 | solution.py:114
  248.5 5.6 fusion.246
  254.1 5.0 exponential_reduce_fusion.3
  259.2 5.6 fusion.246
  264.8 5.0 exponential_reduce_fusion.3
  279.3 8.6 while.18
  279.3 4.3 fusion.252
  288.8 18.7 %all-gather.25.cloned.1.call-done = bf16[768,768]{1,0:T(8,128)(2,1)} async-done(((bf16[96,768]{1,0:T(8,128)(2,1)}), bf16[768,768]{1,0:T(8,128)(2,1)}) %all-gather.25.cloned.1.call-update) | async-done | bytes 1179664 | tf_op jit(solution)/shard_map/all_gather | solution.py:229
  309.6 40.0 %all-gather.27.cloned.1.call-done = bf16[768,768]{1,0:T(8,128)(2,1)} async-done(((bf16[96,768]{1,0:T(8,128)(2,1)}), bf16[768,768]{1,0:T(8,128)(2,1)}) %all-gather.27.cloned.1.call-update) | async-done | bytes 1179664 | tf_op jit(solution)/shard_map/all_gather | solution.py:234
  360.7 30.8 %all-gather.33.cloned.1.call-done = bf16[768,768]{1,0:T(8,128)(2,1)} async-done(((bf16[96,768]{1,0:T(8,128)(2,1)}), bf16[768,768]{1,0:T(8,128)(2,1)}) %all-gather.33.cloned.1.call-update) | async-done | bytes 1179664 | tf_op jit(solution)/shard_map/all_gather | solution.py:237
  393.5 59.4 %all-gather.35.cloned.1.call-done = bf16[768,2048]{1,0:T(8,128)(2,1)} async-done(((bf16[96,2048]{1,0:T(8,128)(2,1)}), bf16[768,2048]{1,0:T(8,128)(2,1)}) %all-gather.35.cloned.1.call-update) | async-done | bytes 3145744 | tf_op jit(solution)/shard_map/all_gather | solution.py:241
  457.2 56.9 %all-gather.37.cloned.1.call-done = bf16[768,2048]{1,0:T(8,128)(2,1)} async-done(((bf16[96,2048]{1,0:T(8,128)(2,1)}), bf16[768,2048]{1,0:T(8,128)(2,1)}) %all-gather.37.cloned.1.call-update) | async-done | bytes 3145744 | tf_op jit(solution)/shard_map/all_gather | solution.py:242
  518.4 57.0 %all-gather.39.cloned.1.call-done = bf16[2048,768]{1,0:T(8,128)(2,1)} async-done(((bf16[256,768]{1,0:T(8,128)(2,1)}), bf16[2048,768]{1,0:T(8,128)(2,1)}) %all-gather.39.cloned.1.call-update) | async-done | bytes 3145744 | tf_op jit(solution)/shard_map/all_gather | solution.py:243
  575.4 6.7 multiply_convert_fusion.1
  590.6 5.1 convolution_convert_fusion.11
  611.9 45.3 %while.19 = (s32[]{:T(128)}, f32[12,256,64]{1,2,0:T(8,128)}, f32[32,12]{0,1:T(8,128)S(1)}, bf16[2,512,12,64]{1,3,2,0:T(8,128)(2,1)}, bf16[2,512,12,64]{1,3,2,0:T...) while((s32[]{:T(128)}, f32[12,256,64]{1,2,0:T(8,128)}, ...), condition=%wide.region_18.19_spmd.clone, body=%wide.region_17.18_spmd.clone.sunk | while | flops 1134035712 | bytes 122996608 | solution.py:181
  630.1 4.5 bitcast_dynamic-update-slice_fusion.5
  652.6 4.4 bitcast_dynamic-update-slice_fusion.5
  680.1 8.7 reduce-scatter.24.cloned.1.call-done
  691.5 28.0 %reduce-scatter.26.cloned.1.call-done = bf16[256,768]{0,1:T(8,128)(2,1)} async-done(((bf16[1024,768]{0,1:T(8,128)(2,1)}), bf16[256,768]{0,1:T(8,128)(2,1)}) %reduce-scatter.26.cloned.1.call-update) | async-done | bytes 393232 | tf_op jit(solution)/shard_map/reduce_scatter | solution.py:413
  743.7 43.2 %reduce-scatter.52.cloned.1.call-done = bf16[96,768]{1,0:T(8,128)(2,1)} async-done(((bf16[768,768]{1,0:T(8,128)(2,1)}), bf16[96,768]{1,0:T(8,128)(2,1)}) %reduce-scatter.52.cloned.1.call-update) | async-done | bytes 147472
  788.6 64.7 %reduce-scatter.50.cloned.1.call-done = bf16[96,768]{1,0:T(8,128)(2,1)} async-done(((bf16[768,768]{1,0:T(8,128)(2,1)}), bf16[96,768]{1,0:T(8,128)(2,1)}) %reduce-scatter.50.cloned.1.call-update) | async-done | bytes 147472
  855.1 64.6 %reduce-scatter.38.cloned.1.call-done = bf16[96,768]{1,0:T(8,128)(2,1)} async-done(((bf16[768,768]{1,0:T(8,128)(2,1)}), bf16[96,768]{1,0:T(8,128)(2,1)}) %reduce-scatter.38.cloned.1.call-update) | async-done | bytes 147472 | tf_op jit(solution)/shard_map/reduce_scatter | solution.py:382
  919.7 66.5 %reduce-scatter.36.cloned.1.call-done = bf16[96,768]{1,0:T(8,128)(2,1)} async-done(((bf16[768,768]{1,0:T(8,128)(2,1)}), bf16[96,768]{1,0:T(8,128)(2,1)}) %reduce-scatter.36.cloned.1.call-update) | async-done | bytes 147472 | tf_op jit(solution)/shard_map/reduce_scatter | solution.py:373
  986.2 66.4 %reduce-scatter.34.cloned.1.call-done = bf16[96,768]{1,0:T(8,128)(2,1)} async-done(((bf16[768,768]{1,0:T(8,128)(2,1)}), bf16[96,768]{1,0:T(8,128)(2,1)}) %reduce-scatter.34.cloned.1.call-update) | async-done | bytes 147472 | tf_op jit(solution)/shard_map/reduce_scatter | solution.py:445
  1052.6 66.6 %reduce-scatter.28.cloned.1.call-done = bf16[96,768]{1,0:T(8,128)(2,1)} async-done(((bf16[768,768]{1,0:T(8,128)(2,1)}), bf16[96,768]{1,0:T(8,128)(2,1)}) %reduce-scatter.28.cloned.1.call-update) | async-done | bytes 147472 | tf_op jit(solution)/shard_map/reduce_scatter | solution.py:436
  1119.1 66.3 %reduce-scatter.30.cloned.1.call-done = bf16[96,768]{1,0:T(8,128)(2,1)} async-done(((bf16[768,768]{1,0:T(8,128)(2,1)}), bf16[96,768]{1,0:T(8,128)(2,1)}) %reduce-scatter.30.cloned.1.call-update) | async-done | bytes 147472 | tf_op jit(solution)/shard_map/reduce_scatter | solution.py:439
  1185.5 66.4 %reduce-scatter.32.cloned.1.call-done = bf16[96,768]{1,0:T(8,128)(2,1)} async-done(((bf16[768,768]{1,0:T(8,128)(2,1)}), bf16[96,768]{1,0:T(8,128)(2,1)}) %reduce-scatter.32.cloned.1.call-update) | async-done | bytes 147472 | tf_op jit(solution)/shard_map/reduce_scatter | solution.py:442
  1251.9 76.8 %reduce-scatter.40.cloned.1.call-done = bf16[96,2048]{1,0:T(8,128)(2,1)} async-done(((bf16[768,2048]{1,0:T(8,128)(2,1)}), bf16[96,2048]{1,0:T(8,128)(2,1)}) %reduce-scatter.40.cloned.1.call-update) | async-done | bytes 393232 | tf_op jit(solution)/shard_map/reduce_scatter | solution.py:315
  1328.7 76.9 %reduce-scatter.42.cloned.1.call-done = bf16[96,2048]{1,0:T(8,128)(2,1)} async-done(((bf16[768,2048]{1,0:T(8,128)(2,1)}), bf16[96,2048]{1,0:T(8,128)(2,1)}) %reduce-scatter.42.cloned.1.call-update) | async-done | bytes 393232 | tf_op jit(solution)/shard_map/reduce_scatter | solution.py:318
  1405.6 77.1 %reduce-scatter.44.cloned.1.call-done = bf16[256,768]{1,0:T(8,128)(2,1)} async-done(((bf16[2048,768]{1,0:T(8,128)(2,1)}), bf16[256,768]{1,0:T(8,128)(2,1)}) %reduce-scatter.44.cloned.1.call-update) | async-done | bytes 393232 | tf_op jit(solution)/shard_map/reduce_scatter | solution.py:321
  1485.3 35.3 %all-reduce.7 = (bf16[768]{0:T(1024)(128)(2,1)S(1)}, bf16[32,12]{1,0:T(8,128)(2,1)S(1)}, bf16[768]{0:T(1024)(128)(2,1)S(1)}, bf16[768]{0:T(1024)(128)(2,1)S(1)}) all-reduce(bf16[768]{0:T(1024)(128)(2,1)S(1)} %get-tuple-element.555, bf16[32,12]{1,0:T(8,128)(2,1)S(1)} %copy.139, ...), channel_id=6, replica_groups=mesh['ctx'=4,'wsh'=8] {'wsh'}, use_global_device_ids=true, to_apply=%region_25.26.clone | all-reduce | flops 2688 | bytes 10752
  1520.9 6.2 all-reduce.9
  1530.3 14.5 all-reduce.13.cloned.1.call-done
  (397 shorter events, 205.4 us)
Async XLA Ops:
  7.2 172.9 %copy-start = (bf16[1,128,768]{2,1,0:T(8,128)(2,1)S(1)}, bf16[1,128,768]{2,1,0:T(8,128)(2,1)}, u32[]{:S(2)}) copy-start(bf16[1,128,768]{2,1,0:T(8,128)(2,1)} %param.28) | copy-start | bytes 589828
  7.2 88.9 %copy-start.12 = (bf16[1,256,768]{2,1,0:T(8,128)(2,1)S(1)}, bf16[1,256,768]{2,1,0:T(8,128)(2,1)}, u32[]{:S(2)}) copy-start(bf16[1,256,768]{2,1,0:T(8,128)(2,1)} %param.27) | copy-start | bytes 1179652
  7.2 46.9 %all-gather.15.cloned.1.call-start = ((), (), s32[]{:S(2)}) async-start(), calls=%async_computation.15 | async-start | bytes 1327104 | tf_op jit(solution)/shard_map/all_gather | solution.py:227
  8.0 88.2 %all-gather.21.cloned.1.call-start = ((), (), s32[]{:S(2)}) async-start(), calls=%async_computation.18 | async-start | bytes 1327104 | tf_op jit(solution)/shard_map/all_gather | solution.py:228
  8.7 141.6 %all-gather.19.cloned.1.call-start = ((), (), s32[]{:S(2)}) async-start(), calls=%async_computation.17 | async-start | bytes 1327104 | tf_op jit(solution)/shard_map/all_gather | solution.py:226
  9.4 170.7 %all-gather.29.cloned.1.call-start = ((), (), s32[]{:S(2)}) async-start(), calls=%async_computation.22 | async-start | bytes 1327104 | tf_op jit(solution)/shard_map/all_gather | solution.py:235
  10.0 212.0 %all-gather.31.cloned.1.call-start = ((), (), s32[]{:S(2)}) async-start(), calls=%async_computation.23 | async-start | bytes 1327104 | tf_op jit(solution)/shard_map/all_gather | solution.py:236
  10.6 231.9 %all-gather.17.cloned.1.call-start = ((), (), s32[]{:S(2)}) async-start(), calls=%async_computation.16 | async-start | bytes 1966080 | tf_op jit(solution)/shard_map/all_gather | solution.py:262
  38.6 111.7 %copy-start.64 = (f32[768]{0:T(1024)}, f32[768]{0:T(1024)S(1)}, u32[]{:S(2)}) copy-start(f32[768]{0:T(1024)S(1)} %convert_element_type.546) | copy-start | bytes 9220
  40.3 110.0 %copy-start.72 = (f32[256]{0:T(256)}, f32[256]{0:T(256)S(1)}, u32[]{:S(2)}) copy-start(f32[256]{0:T(256)S(1)} %get-tuple-element.649) | copy-start | bytes 3076
  56.7 46.2 %copy-start.76 = (s32[1,8]{1,0:T(1,128)S(1)}, s32[1,8]{1,0:T(1,128)}, u32[]{:S(2)}) copy-start(s32[1,8]{1,0:T(1,128)} %param.29) | copy-start | bytes 100
  56.7 46.5 %copy-start.75 = (bf16[4,12]{1,0:T(4,128)(2,1)S(1)}, bf16[4,12]{1,0:T(4,128)(2,1)}, u32[]{:S(2)}) copy-start(bf16[4,12]{1,0:T(4,128)(2,1)} %param.36) | copy-start | bytes 292
  56.8 213.1 %all-gather.23.cloned.1.call-start = ((), (), s32[]{:S(2)}) async-start(), calls=%async_computation.19 | async-start | bytes 1966080 | tf_op jit(solution)/shard_map/all_gather | solution.py:263
  98.7 208.9 %all-gather.25.cloned.1.call-start = ((), (), s32[]{:S(2)}) async-start(), calls=%async_computation.20 | async-start | bytes 1327104 | tf_op jit(solution)/shard_map/all_gather | solution.py:229
  99.4 250.2 %all-gather.27.cloned.1.call-start = ((), (), s32[]{:S(2)}) async-start(), calls=%async_computation.21 | async-start | bytes 1327104 | tf_op jit(solution)/shard_map/all_gather | solution.py:234
  100.2 291.4 %all-gather.33.cloned.1.call-start = ((), (), s32[]{:S(2)}) async-start(), calls=%async_computation.24 | async-start | bytes 1327104 | tf_op jit(solution)/shard_map/all_gather | solution.py:237
  100.7 352.2 %all-gather.35.cloned.1.call-start = ((), (), s32[]{:S(2)}) async-start(), calls=%async_computation.25 | async-start | bytes 3538944 | tf_op jit(solution)/shard_map/all_gather | solution.py:241
  101.5 412.6 %all-gather.37.cloned.1.call-start = ((), (), s32[]{:S(2)}) async-start(), calls=%async_computation.26 | async-start | bytes 3538944 | tf_op jit(solution)/shard_map/all_gather | solution.py:242
  102.1 473.3 %all-gather.39.cloned.1.call-start = ((), (), s32[]{:S(2)}) async-start(), calls=%async_computation.27 | async-start | bytes 3538944 | tf_op jit(solution)/shard_map/all_gather | solution.py:243
  102.8 563.7 %reduce-scatter.48.cloned.1.call-start = ((), (), s32[]{:S(2)}) async-start(), calls=%async_computation.40 | async-start | bytes 983040
  279.3 28.3 %copy-start.13 = (bf16[1,256,768]{2,1,0:T(8,128)(2,1)S(1)}, bf16[1,256,768]{2,1,0:T(8,128)(2,1)}, u32[]{:S(2)}) copy-start(bf16[1,256,768]{2,1,0:T(8,128)(2,1)} %param.27) | copy-start | bytes 1179652
  287.9 19.6 %copy-start.46 = (f32[12,256,64]{1,2,0:T(8,128)}, f32[12,256,64]{1,2,0:T(8,128)S(1)}, u32[]{:S(2)}) copy-start(f32[12,256,64]{1,2,0:T(8,128)S(1)} %get-tuple-element.256) | copy-start | bytes 2359300
  288.0 64.2 %copy-start.4 = (bf16[2,512,12,64]{1,3,2,0:T(8,128)(2,1)}, bf16[2,512,12,64]{1,3,2,0:T(8,128)(2,1)S(1)}, u32[]{:S(2)}) copy-start(bf16[2,512,12,64]{1,3,2,0:T(8,128)(2,1)S(1)} %get-tuple-element.1039) | copy-start | bytes 4718596
  309.6 299.3 %copy-start.9 = (f32[256,768]{1,0:T(8,128)}, f32[256,768]{1,0:T(8,128)S(1)}, u32[]{:S(2)}) copy-start(f32[256,768]{1,0:T(8,128)S(1)} %get-tuple-element.659) | copy-start | bytes 2359300
  360.7 32.7 %copy-start.39 = (bf16[12,256,64]{1,2,0:T(8,128)(2,1)}, bf16[12,256,64]{1,2,0:T(8,128)(2,1)S(1)}, u32[]{:S(2)}) copy-start(bf16[12,256,64]{1,2,0:T(8,128)(2,1)S(1)} %get-tuple-element.662) | copy-start | bytes 1179652
  393.4 192.7 %copy-start.18 = (f32[256,768]{1,0:T(8,128)}, f32[256,768]{1,0:T(8,128)S(1)}, u32[]{:S(2)}) copy-start(f32[256,768]{1,0:T(8,128)S(1)} %get-tuple-element.665) | copy-start | bytes 2359300
  393.5 120.6 %copy-start.15 = (bf16[256,768]{1,0:T(8,128)(2,1)}, bf16[256,768]{1,0:T(8,128)(2,1)S(1)}, u32[]{:S(2)}) copy-start(bf16[256,768]{1,0:T(8,128)(2,1)S(1)} %multiply_convert_fusion.3) | copy-start | bytes 1179652
  457.2 118.2 %copy-start.51 = (bf16[1,256,768]{2,1,0:T(8,128)(2,1)S(1)}, bf16[1,256,768]{2,1,0:T(8,128)(2,1)}, u32[]{:S(2)}) copy-start(bf16[1,256,768]{2,1,0:T(8,128)(2,1)} %param.30) | copy-start | bytes 1179652
  601.2 68.3 %reduce-scatter.46.cloned.1.call-start = ((), (), s32[]{:S(2)}) async-start(), calls=%async_computation.39 | async-start | bytes 983040
  611.8 77.0 %reduce-scatter.24.cloned.1.call-start = ((), (), s32[]{:S(2)}) async-start(), calls=%async_computation.28 | async-start | bytes 1966080 | tf_op jit(solution)/shard_map/reduce_scatter | solution.py:410
  661.8 57.8 %reduce-scatter.26.cloned.1.call-start = ((), (), s32[]{:S(2)}) async-start(), calls=%async_computation.29 | async-start | bytes 1966080 | tf_op jit(solution)/shard_map/reduce_scatter | solution.py:413
  666.4 120.5 %reduce-scatter.52.cloned.1.call-start = ((), (), s32[]{:S(2)}) async-start(), calls=%async_computation.42 | async-start | bytes 1327104
  669.5 183.9 %reduce-scatter.50.cloned.1.call-start = ((), (), s32[]{:S(2)}) async-start(), calls=%async_computation.41 | async-start | bytes 1327104
  672.5 247.2 %reduce-scatter.38.cloned.1.call-start = ((), (), s32[]{:S(2)}) async-start(), calls=%async_computation.35 | async-start | bytes 1327104 | tf_op jit(solution)/shard_map/reduce_scatter | solution.py:382
  674.1 312.0 %reduce-scatter.36.cloned.1.call-start = ((), (), s32[]{:S(2)}) async-start(), calls=%async_computation.34 | async-start | bytes 1327104 | tf_op jit(solution)/shard_map/reduce_scatter | solution.py:373
  675.9 376.7 %reduce-scatter.34.cloned.1.call-start = ((), (), s32[]{:S(2)}) async-start(), calls=%async_computation.33 | async-start | bytes 1327104 | tf_op jit(solution)/shard_map/reduce_scatter | solution.py:445
  677.5 441.6 %reduce-scatter.28.cloned.1.call-start = ((), (), s32[]{:S(2)}) async-start(), calls=%async_computation.30 | async-start | bytes 1327104 | tf_op jit(solution)/shard_map/reduce_scatter | solution.py:436
  680.0 505.5 %reduce-scatter.30.cloned.1.call-start = ((), (), s32[]{:S(2)}) async-start(), calls=%async_computation.31 | async-start | bytes 1327104 | tf_op jit(solution)/shard_map/reduce_scatter | solution.py:439
  691.5 30.8 %copy-start.16 = (bf16[256,768]{1,0:T(8,128)(2,1)S(1)}, bf16[256,768]{1,0:T(8,128)(2,1)}, u32[]{:S(2)}) copy-start(bf16[256,768]{1,0:T(8,128)(2,1)} %copy-done.15) | copy-start | bytes 1179652
  691.5 30.8 %copy-start.58 = (bf16[256,2048]{1,0:T(8,128)(2,1)S(1)}, bf16[256,2048]{1,0:T(8,128)(2,1)}, u32[]{:S(2)}) copy-start(bf16[256,2048]{1,0:T(8,128)(2,1)} %copy-done.57) | copy-start | bytes 3145732
  691.5 560.4 %reduce-scatter.32.cloned.1.call-start = ((), (), s32[]{:S(2)}) async-start(), calls=%async_computation.32 | async-start | bytes 1327104 | tf_op jit(solution)/shard_map/reduce_scatter | solution.py:442
  722.2 606.5 %reduce-scatter.40.cloned.1.call-start = ((), (), s32[]{:S(2)}) async-start(), calls=%async_computation.36 | async-start | bytes 3538944 | tf_op jit(solution)/shard_map/reduce_scatter | solution.py:315
  725.0 680.6 %reduce-scatter.42.cloned.1.call-start = ((), (), s32[]{:S(2)}) async-start(), calls=%async_computation.37 | async-start | bytes 3538944 | tf_op jit(solution)/shard_map/reduce_scatter | solution.py:318
  728.9 753.8 %reduce-scatter.44.cloned.1.call-start = ((), (), s32[]{:S(2)}) async-start(), calls=%async_computation.38 | async-start | bytes 3538944 | tf_op jit(solution)/shard_map/reduce_scatter | solution.py:321
  733.1 811.8 %all-reduce.13.cloned.1.call-start = ((), (), s32[]{:S(2)}) async-start(), calls=%async_computation.43 | async-start | bytes 4915200 | tf_op jit(solution)/shard_map/psum | solution.py:461
  742.5 740.3 %copy-start.49 = (f32[256,768]{1,0:T(8,128)S(1)}, f32[256,768]{1,0:T(8,128)}, u32[]{:S(2)}) copy-start(f32[256,768]{1,0:T(8,128)} %fusion.151) | copy-start | bytes 2359300
  742.5 740.3 %copy-start.54 = (bf16[256,768]{0,1:T(8,128)(2,1)S(1)}, bf16[256,768]{0,1:T(8,128)(2,1)}, u32[]{:S(2)}) copy-start(bf16[256,768]{0,1:T(8,128)(2,1)} %reduce-scatter.24.cloned.1.call-done) | copy-start | bytes 1179652
  1484.7 44.5 %copy-start.74 = (f32[256]{0:T(256)S(1)}, f32[256]{0:T(256)}, u32[]{:S(2)}) copy-start(f32[256]{0:T(256)} %get-tuple-element.648) | copy-start | bytes 3076
  (70 other events, 235.4 us)
Sparse Core Ops, SparseCore 0:
  10.2 43.7 all-gather.14
  56.2 39.8 all-gather.20
  98.3 39.8 all-gather.18
  140.3 39.8 all-gather.28
  182.2 39.8 all-gather.30
  224.0 18.4 all-gather.16
  244.6 19.6 all-gather.22
  266.5 41.0 all-gather.24
  309.8 39.8 all-gather.26
  351.6 39.8 all-gather.32
  393.7 59.2 all-gather.34
  455.0 59.0 all-gather.36
  516.3 59.0 all-gather.38
  601.3 21.8 reduce-scatter.47
  626.3 23.2 reduce-scatter.45
  661.9 26.8 reduce-scatter.23
  691.4 28.1 reduce-scatter.25
  722.8 64.0 reduce-scatter.51
  790.3 63.0 reduce-scatter.49
  856.6 63.0 reduce-scatter.37
  923.1 63.0 reduce-scatter.35
  989.6 62.9 reduce-scatter.33
  1056.0 63.1 reduce-scatter.27
  1122.4 63.0 reduce-scatter.29
  1188.9 63.0 reduce-scatter.31
  1255.4 73.2 reduce-scatter.39
  1332.1 73.3 reduce-scatter.41
  1409.1 73.4 reduce-scatter.43
  1486.4 58.3 all-reduce.12
where the time goes:
time: 1570 us; the launch traced here: 1560 us
  waiting for transfers between devices  1180 us (75%)
  matrix products  159 us (10%)
  blocking collectives  100 us (6%)
  local copies, waits for them, and re-layouts  74.1 us (5%)
  other arithmetic  31.8 us (2%)
  between operations  17.3 us (1%)
    unnamed x33, waiting for transfers between devices  115 us
    reduce_scatter x1, waiting for transfers between devices, on_device(): lax.psum_scatter(down_part.astype(jnp.bfloat16), 'wsh', scatter_dimension...  77.1 us
    reduce_scatter x1, waiting for transfers between devices, on_device(): lax.psum_scatter(up_part.astype(jnp.bfloat16), 'wsh', scatter_dimension=0...  76.9 us
    reduce_scatter x1, waiting for transfers between devices, on_device(): lax.psum_scatter(gate_part.astype(jnp.bfloat16), 'wsh', scatter_dimension...  76.8 us
    reduce_scatter x1, waiting for transfers between devices, on_device(): lax.psum_scatter(query_self_part.astype(jnp.bfloat16), 'wsh', scatter_dim...  66.6 us
    reduce_scatter x1, waiting for transfers between devices, on_device(): lax.psum_scatter(query_cross_part.astype(jnp.bfloat16), 'wsh', scatter_di...  66.5 us
    reduce_scatter x1, waiting for transfers between devices, on_device(): lax.psum_scatter(value_self_part.astype(jnp.bfloat16), 'wsh', scatter_dim...  66.4 us
    reduce_scatter x1, waiting for transfers between devices, on_device(): lax.psum_scatter(output_self_part.astype(jnp.bfloat16), 'wsh', scatter_di...  66.4 us
  transfers between devices with their start and end apart: 29, of which 25 were waited for; matrix products, arithmetic and copies ran while one was open for 14% of the time, Pallas kernels for 0%

commit v1 on v0

v1 whole, which is shorter than its diff:
```python
import math

import jax
import jax.numpy as jnp
from jax import lax
from jax.sharding import PartitionSpec as P

norm_eps = 1e-06
neg_big = -1000000000.0


def bucket_index(distance):
    counter = jnp.zeros_like(distance)
    for number in range(1, 16):
        threshold = math.ceil(16 * 8 ** (number / 16))
        counter = counter + (distance >= threshold).astype(distance.dtype)
    return jnp.where(distance < 16, distance, 16 + counter)


def gelu_tanh(values):
    return jax.nn.gelu(values, approximate=True)


def rms_forward(values, gain_vec):
    inv_rms = lax.rsqrt(jnp.mean(values * values, axis=-1, keepdims=True) + norm_eps)
    return (values * inv_rms * gain_vec, inv_rms)


def rms_backward(values, inv_rms, gain_vec, normalized_grad):
    weighted = normalized_grad * gain_vec
    gain_grad = jnp.sum(normalized_grad * values * inv_rms, axis=0)
    inner_mean = jnp.mean(weighted * values, axis=-1, keepdims=True)
    return (inv_rms * weighted - values * (inv_rms * inv_rms * inv_rms) * inner_mean, gain_grad)


def matmul(left_side, right_side):
    return jnp.dot(left_side, right_side, preferred_element_type=jnp.float32)


def matmul_tn(left_side, right_side):
    return lax.dot_general(
        left_side, right_side, (((0,), (0,)), ((), ())), preferred_element_type=jnp.float32
    )


def matmul_nt(left_side, right_side):
    return lax.dot_general(
        left_side, right_side, (((1,), (1,)), ((), ())), preferred_element_type=jnp.float32
    )


def split_heads(matrix, head_count):
    return jnp.transpose(matrix.reshape(matrix.shape[0], head_count, -1), (1, 0, 2))


def join_heads(tensor):
    return jnp.transpose(tensor, (1, 0, 2)).reshape(tensor.shape[1], -1)


def bucket_onehot(query_pos, key_pos, bucket_count):
    distance = query_pos[:, None] - key_pos[None, :]
    buckets = bucket_index(jnp.maximum(distance, 0))
    selection_flag = (
        buckets[None] == jnp.arange(bucket_count, dtype=buckets.dtype)[:, None, None]
    ).astype(jnp.bfloat16)
    return (selection_flag, distance >= 0)


def self_bias_maker(query_pos, entire_position_bias_table, bucket_count):

    def maker(key_pos):
        selection_flag, allowed = bucket_onehot(query_pos, key_pos, bucket_count)
        bias_tile = jnp.einsum(
            "dvc,dz->zvc",
            selection_flag,
            entire_position_bias_table,
            preferred_element_type=jnp.float32,
        )
        return (bias_tile, allowed, selection_flag)

    return maker


def masked_bias_tiles(query_pos, key_marks, entire_position_bias_table, bucket_count):
    maker = self_bias_maker(query_pos, entire_position_bias_table, bucket_count)

    def one_tile(key_pos):
        bias_tile, allowed, unused = maker(key_pos)
        return jnp.where(allowed[None], bias_tile, neg_big).astype(jnp.bfloat16)

    return lax.map(one_tile, key_marks)


def score_tile(query_heads, key_tile, bias_tile):
    scores = jnp.einsum("hqd,khd->hqk", query_heads, key_tile, preferred_element_type=jnp.float32)
    if bias_tile is None:
        return scores
    return scores + bias_tile.astype(jnp.float32)


def attend_forward(query_heads, key_tiles, value_tiles, bias_tiles):
    row_shape = (query_heads.shape[0], query_heads.shape[1])

    def measure(carry, slices):
        row_max, row_total = carry
        scores = score_tile(query_heads, slices[0], slices[1])
        new_max = jnp.maximum(row_max, jnp.max(scores, axis=-1))
        row_total = row_total * jnp.exp(row_max - new_max) + jnp.sum(
            jnp.exp(scores - new_max[..., None]), axis=-1
        )
        return ((new_max, row_total), None)

    initial = (jnp.full(row_shape, neg_big, jnp.float32), jnp.zeros(row_shape, jnp.float32))
    (row_max, row_total), unused = lax.scan(measure, initial, (key_tiles, bias_tiles))
    log_total = row_max + jnp.log(row_total)

    def collect(running, slices):
        scores = score_tile(query_heads, slices[0], slices[2])
        weights = jnp.exp(scores - log_total[..., None]).astype(jnp.bfloat16)
        return (
            running
            + jnp.einsum("hqk,khd->hqd", weights, slices[1], preferred_element_type=jnp.float32),
            None,
        )

    blended, unused = lax.scan(
        collect, jnp.zeros(query_heads.shape, jnp.float32), (key_tiles, value_tiles, bias_tiles)
    )
    return (blended, log_total)


def attend_backward(
    query_heads,
    key_tiles,
    value_tiles,
    bias_tiles,
    key_marks,
    query_pos,
    log_total,
    output_grad,
    blended,
    bucket_count,
):
    delta_rows = jnp.sum(output_grad.astype(jnp.float32) * blended, axis=-1)

    def sweep(carry, slices):
        query_grad, table_grad = carry
        key_tile, value_tile, bias_tile, marks = slices
        scores = score_tile(query_heads, key_tile, bias_tile)
        probs = jnp.exp(scores - log_total[..., None])
        probs_grad = jnp.einsum(
            "hqd,khd->hqk", output_grad, value_tile, preferred_element_type=jnp.float32
        )
        gradient_of_scores = (probs * (probs_grad - delta_rows[..., None])).astype(jnp.bfloat16)
        query_grad = query_grad + jnp.einsum(
            "hqk,khd->hqd", gradient_of_scores, key_tile, preferred_element_type=jnp.float32
        )
        if bias_tile is not None:
            selection_flag, unused = bucket_onehot(query_pos, marks, bucket_count)
            table_grad = table_grad + jnp.einsum(
                "exo,dxo->ed",
                selection_flag,
                gradient_of_scores,
                preferred_element_type=jnp.float32,
            )
        key_grad = jnp.einsum(
            "hqk,hqd->khd", gradient_of_scores, query_heads, preferred_element_type=jnp.float32
        )
        value_grad = jnp.einsum(
            "hqk,hqd->khd",
            probs.astype(jnp.bfloat16),
            output_grad,
            preferred_element_type=jnp.float32,
        )
        return ((query_grad, table_grad), (key_grad, value_grad))

    initial = (
        jnp.zeros(query_heads.shape, jnp.float32),
        jnp.zeros((bucket_count, query_heads.shape[0]), jnp.float32),
    )
    (query_grad, table_grad), key_side = lax.scan(
        sweep, initial, (key_tiles, value_tiles, bias_tiles, key_marks)
    )
    key_grads, value_grads = key_side
    key_total = key_grads.shape[0] * key_grads.shape[1]
    return (
        query_grad,
        key_grads.reshape(key_total, -1),
        value_grads.reshape(key_total, -1),
        table_grad,
        delta_rows,
    )


def exchange(block, axis, bit):
    count = lax.axis_size(axis)
    return lax.ppermute(block, axis, [(i, i ^ bit) for i in range(count)])


def bits_of(axis):
    bit, bits = lax.axis_size(axis) // 2, []
    while bit:
        bits.append(bit)
        bit //= 2
    return bits


def gather_over(block, axis):
    index = lax.axis_index(axis)
    held = block[None]
    for bit in bits_of(axis):
        other = exchange(held, axis, bit)
        upper = (index & bit) != 0
        pair = [jnp.where(upper, other, held), jnp.where(upper, held, other)]
        held = jnp.stack(pair, axis=1).reshape((-1,) + block.shape)
    return held


def spread_over(block, axis):
    index = lax.axis_index(axis)
    held = [(0, block)]
    for bit in bits_of(axis):
        held = held + [(offset ^ bit, exchange(piece, axis, bit)) for offset, piece in held]
    joined = jnp.zeros((lax.axis_size(axis),) + block.shape, block.dtype)
    for offset, piece in held:
        joined = lax.dynamic_update_slice_in_dim(joined, piece[None], index ^ offset, 0)
    return joined


def gather_weights(block):
    return spread_over(gather_over(block, "wsh"), "ctx")


def reduce_steps(parts, order, ctx_dim, wsh_dim):
    shape = list(parts.shape)
    names, split = [], []
    for dim, size in enumerate(shape):
        if dim == ctx_dim or dim == wsh_dim:
            axis = "ctx" if dim == ctx_dim else "wsh"
            for bit in bits_of(axis):
                names.append((axis, bit))
                split.append(2)
        else:
            names.append(None)
            split.append(size)
    held = parts.astype(jnp.bfloat16).reshape(split)
    for axis, bit in order:
        dim = names.index((axis, bit))
        mine = ((lax.axis_index(axis) & bit) != 0).astype(jnp.int32)
        away = lax.dynamic_index_in_dim(held, 1 - mine, dim, keepdims=False)
        kept = lax.dynamic_index_in_dim(held, mine, dim, keepdims=False)
        came = exchange(away, axis, bit)
        held = (kept.astype(jnp.float32) + came.astype(jnp.float32)).astype(jnp.bfloat16)
        names.pop(dim)
    return held


def reduce_order(first):
    ctx = [("ctx", bit) for bit in reversed(bits_of("ctx"))]
    wsh = [("wsh", bit) for bit in reversed(bits_of("wsh"))]
    if first == "ctx":
        return ctx + wsh
    return ctx[:1] + wsh[:1] + ctx[1:] + wsh[1:]


def reduce_ctx(parts):
    size = lax.axis_size("ctx")
    blocks = parts.reshape((size, parts.shape[0] // size) + parts.shape[1:])
    return reduce_steps(blocks, [("ctx", bit) for bit in reversed(bits_of("ctx"))], 0, None)


def square_pieces(shards):
    size = lax.axis_size("ctx")
    rows = jnp.concatenate(shards, axis=0)
    step = rows.shape[0] // size
    return lax.dynamic_slice_in_dim(rows, lax.axis_index("ctx") * step, step)


def square_join(pieces, count):
    ctx, wsh, step, width = pieces.shape
    if ctx == count:
        return [pieces[k].reshape(-1, width) for k in range(count)]
    moved = jnp.transpose(pieces, (1, 0, 2, 3)).reshape(wsh, count, -1, width)
    return [moved[:, k].reshape(-1, width) for k in range(count)]


def square_reduce(parts, first):
    ctx, wsh, count = lax.axis_size("ctx"), lax.axis_size("wsh"), len(parts)
    stacked = jnp.stack([part.astype(jnp.bfloat16) for part in parts])
    width = stacked.shape[-1]
    if ctx == count:
        stacked = stacked.reshape(ctx, wsh, -1, width)
    else:
        stacked = stacked.reshape(count, wsh, -1, width).transpose(1, 0, 2, 3)
        stacked = stacked.reshape(wsh, ctx, -1, width).transpose(1, 0, 2, 3)
    owned = spread_over(reduce_steps(stacked, reduce_order(first), 0, 1), "ctx")
    owned = owned.reshape(count, -1, width).astype(jnp.float32)
    return [owned[k] for k in range(count)]


def small_reduce(parts):
    for bit in bits_of("ctx"):
        parts = parts + exchange(parts, "ctx", bit)
    for bit in bits_of("wsh"):
        half = parts.shape[0] // 2
        mine = ((lax.axis_index("wsh") & bit) != 0).astype(jnp.int32)
        pair = parts.reshape(2, half, -1)
        away = lax.dynamic_index_in_dim(pair, 1 - mine, 0, keepdims=False)
        kept = lax.dynamic_index_in_dim(pair, mine, 0, keepdims=False)
        parts = kept + exchange(away, "wsh", bit)
    return parts[0]


def on_device(
    layer_input,
    encoder_states,
    block_order,
    out_grad,
    self_gain,
    query_self,
    key_self,
    value_self,
    output_self,
    bias_table,
    cross_gain,
    cross_query_weight,
    key_cross,
    value_cross,
    output_cross,
    ffn_gain,
    ffn_gate,
    ffn_up,
    ffn_down,
):
    head_count = bias_table.shape[1]
    wsh_size = lax.axis_size("wsh")
    ctx_size = lax.axis_size("ctx")
    bucket_count = bias_table.shape[0] * wsh_size
    row_count = layer_input.shape[1]
    seq_total = row_count * ctx_size
    block_rows = seq_total // block_order.shape[1]
    key_block = math.gcd(seq_total, 512)
    enc_total = encoder_states.shape[1] * ctx_size
    encoder_block_rows = math.gcd(enc_total, 512)
    ctx_index = lax.axis_index("ctx")
    model_width = layer_input.shape[2]
    head_size = model_width // head_count
    gain_rows = self_gain.shape[0]

    small = gather_over(
        jnp.concatenate([self_gain, cross_gain, ffn_gain, bias_table.reshape(-1)]), "wsh"
    )
    gain_one = small[:, :gain_rows].reshape(-1).astype(jnp.float32)
    gain_two = small[:, gain_rows : 2 * gain_rows].reshape(-1).astype(jnp.float32)
    gain_three = small[:, 2 * gain_rows : 3 * gain_rows].reshape(-1).astype(jnp.float32)
    table = small[:, 3 * gain_rows :].reshape(bucket_count, head_count)

    w_query, w_key, w_value, w_out = square_join(
        gather_weights(square_pieces([query_self, key_self, value_self, output_self])), 4
    )
    x_query, x_key, x_value, x_out = square_join(
        gather_weights(square_pieces([cross_query_weight, key_cross, value_cross, output_cross])),
        4,
    )
    wide = jnp.concatenate([ffn_gate, ffn_up], axis=1)
    wide_step = wide.shape[1] // ctx_size
    wide = gather_weights(
        lax.dynamic_slice_in_dim(wide, ctx_index * wide_step, wide_step, axis=1)
    ).reshape(ctx_size, model_width, wide_step)
    down_step = ffn_down.shape[0] // ctx_size
    down = gather_weights(lax.dynamic_slice_in_dim(ffn_down, ctx_index * down_step, down_step))
    down = jnp.transpose(down, (1, 0, 2, 3)).reshape(-1, wide_step, model_width)
    half = ctx_size // 2

    order_row = block_order[0]
    key_pos = (
        order_row[:, None] * block_rows + jnp.arange(block_rows, dtype=jnp.int32)[None, :]
    ).reshape(-1)
    query_pos = lax.dynamic_slice_in_dim(key_pos, ctx_index * row_count, row_count)
    self_marks = key_pos.reshape(-1, key_block)
    inputs_now = layer_input[0].astype(jnp.float32)
    normed_one, inv_one = rms_forward(inputs_now, gain_one)
    normed_one = normed_one.astype(jnp.bfloat16)
    keys_one = matmul(normed_one, w_key).astype(jnp.bfloat16)
    values_one = matmul(normed_one, w_value).astype(jnp.bfloat16)
    keys_all = spread_over(keys_one, "ctx")
    values_all = spread_over(values_one, "ctx")
    queries_one = matmul(normed_one, w_query).astype(jnp.bfloat16)
    encoder_rows = encoder_states[0]
    keys_far = spread_over(matmul(encoder_rows, x_key).astype(jnp.bfloat16), "ctx")
    values_far = spread_over(matmul(encoder_rows, x_value).astype(jnp.bfloat16), "ctx")
    keys_self_attention = keys_all.reshape(-1, key_block, head_count, head_size)
    self_values = values_all.reshape(-1, key_block, head_count, head_size)
    cross_keys = keys_far.reshape(-1, encoder_block_rows, head_count, head_size)
    cross_values = values_far.reshape(-1, encoder_block_rows, head_count, head_size)
    heads_one = split_heads(queries_one, head_count)
    self_bias = masked_bias_tiles(query_pos, self_marks, table, bucket_count)
    blended_one, log_one = attend_forward(heads_one, keys_self_attention, self_values, self_bias)
    attn_self = join_heads(blended_one).astype(jnp.bfloat16)
    section_two = inputs_now + matmul(attn_self, w_out)
    normed_two, inv_two = rms_forward(section_two, gain_two)
    normed_two = normed_two.astype(jnp.bfloat16)
    queries_two = matmul(normed_two, x_query).astype(jnp.bfloat16)
    heads_two = split_heads(queries_two, head_count)
    blended_two, log_two = attend_forward(heads_two, cross_keys, cross_values, None)
    attn_cross = join_heads(blended_two).astype(jnp.bfloat16)
    section_three = section_two + matmul(attn_cross, x_out)
    normed_three, inv_three = rms_forward(section_three, gain_three)
    normed_three = normed_three.astype(jnp.bfloat16)

    grad_now = out_grad[0].astype(jnp.float32)
    grad_three = out_grad[0]
    result = section_three
    normed_three_grad = jnp.zeros_like(section_three)
    gate_parts, up_parts, down_parts = [], [], []
    for k in range(half):
        gate_pre = matmul(normed_three, wide[k])
        up_pre = matmul(normed_three, wide[half + k])
        activated, gelu_pull = jax.vjp(gelu_tanh, gate_pre)
        hidden = (activated * up_pre).astype(jnp.bfloat16)
        result = result + matmul(hidden, down[k])
        hidden_grad = matmul_nt(grad_three, down[k])
        gate_grad = gelu_pull(hidden_grad * up_pre)[0].astype(jnp.bfloat16)
        up_grad = (hidden_grad * activated).astype(jnp.bfloat16)
        normed_three_grad = (
            normed_three_grad + matmul_nt(gate_grad, wide[k]) + matmul_nt(up_grad, wide[half + k])
        )
        gate_parts.append(matmul_tn(normed_three, gate_grad).astype(jnp.bfloat16))
        up_parts.append(matmul_tn(normed_three, up_grad).astype(jnp.bfloat16))
        down_parts.append(matmul_tn(hidden, grad_three).astype(jnp.bfloat16))
    result = result.astype(jnp.bfloat16)
    extra_three, ffn_gain_part = rms_backward(
        section_three, inv_three, gain_three, normed_three_grad
    )
    section_three_grad = grad_now + extra_three
    wide_parts = jnp.stack(gate_parts + up_parts).reshape(ctx_size, wsh_size, -1, wide_step)
    wide_own = spread_over(reduce_steps(wide_parts, reduce_order("ctx"), 0, 1), "ctx")
    wide_own = jnp.transpose(wide_own, (1, 0, 2)).reshape(wide_own.shape[1], -1)
    wide_own = wide_own.astype(jnp.float32)
    down_rows = jnp.stack(down_parts).reshape(wsh_size, ctx_size, -1, model_width)
    down_own = spread_over(reduce_steps(down_rows, reduce_order("wsh"), 1, 0), "ctx")
    down_own = down_own.reshape(-1, model_width).astype(jnp.float32)

    branch_two_grad = section_three_grad.astype(jnp.bfloat16)
    output_cross_part = matmul_tn(attn_cross, branch_two_grad)
    attn_cross_grad = matmul_nt(branch_two_grad, x_out).astype(jnp.bfloat16)
    query_two_grad, far_key_grad, far_value_grad, unused, unused_delta = attend_backward(
        heads_two,
        cross_keys,
        cross_values,
        None,
        None,
        query_pos,
        log_two,
        split_heads(attn_cross_grad, head_count),
        blended_two,
        1,
    )
    far_key_low = reduce_ctx(far_key_grad)
    far_value_low = reduce_ctx(far_value_grad)
    query_two_low = join_heads(query_two_grad).astype(jnp.bfloat16)
    query_cross_part = matmul_tn(normed_two, query_two_low)
    normed_two_grad = matmul_nt(query_two_low, x_query)
    extra_two, cross_gain_part = rms_backward(section_two, inv_two, gain_two, normed_two_grad)
    section_two_grad = section_three_grad + extra_two
    key_cross_part = matmul_tn(encoder_rows, far_key_low)
    value_cross_part = matmul_tn(encoder_rows, far_value_low)
    encoder_state_gradient = matmul_nt(far_key_low, x_key) + matmul_nt(far_value_low, x_value)
    cross_own = square_reduce(
        [query_cross_part, key_cross_part, value_cross_part, output_cross_part], "wsh"
    )

    branch_one_grad = section_two_grad.astype(jnp.bfloat16)
    output_self_part = matmul_tn(attn_self, branch_one_grad)
    attn_self_grad = matmul_nt(branch_one_grad, w_out).astype(jnp.bfloat16)
    query_one_grad, own_key_grad, own_value_grad, table_part, delta_one = attend_backward(
        heads_one,
        keys_self_attention,
        self_values,
        self_bias,
        self_marks,
        query_pos,
        log_one,
        split_heads(attn_self_grad, head_count),
        blended_one,
        bucket_count,
    )
    own_key_low = reduce_ctx(own_key_grad)
    own_value_low = reduce_ctx(own_value_grad)
    query_one_low = join_heads(query_one_grad).astype(jnp.bfloat16)
    query_self_part = matmul_tn(normed_one, query_one_low)
    key_self_part = matmul_tn(normed_one, own_key_low)
    value_self_part = matmul_tn(normed_one, own_value_low)
    self_own = square_reduce(
        [query_self_part, key_self_part, value_self_part, output_self_part], "ctx"
    )
    normed_one_grad = (
        matmul_nt(query_one_low, w_query)
        + matmul_nt(own_key_low, w_key)
        + matmul_nt(own_value_low, w_value)
    )
    additional_first, self_gain_part = rms_backward(inputs_now, inv_one, gain_one, normed_one_grad)
    input_grad = section_two_grad + additional_first
    small_own = small_reduce(
        jnp.concatenate(
            [
                self_gain_part.reshape(wsh_size, -1),
                cross_gain_part.reshape(wsh_size, -1),
                ffn_gain_part.reshape(wsh_size, -1),
                table_part.reshape(wsh_size, -1),
            ],
            axis=1,
        )
    )
    ff_width = ffn_gate.shape[1]
    return (
        result[None],
        input_grad[None],
        encoder_state_gradient[None],
        small_own[:gain_rows],
        self_own[0],
        self_own[1],
        self_own[2],
        self_own[3],
        small_own[3 * gain_rows :].reshape(bias_table.shape),
        small_own[gain_rows : 2 * gain_rows],
        cross_own[0],
        cross_own[1],
        cross_own[2],
        cross_own[3],
        small_own[2 * gain_rows : 3 * gain_rows],
        wide_own[:, :ff_width],
        wide_own[:, ff_width:],
        down_own,
    )


def solution(mesh):
    in_specs = (
        P("wsh", "ctx", None),
        P("wsh", "ctx", None),
        P("wsh", None),
        P("wsh", "ctx", None),
        P("wsh"),
        P("wsh", None),
        P("wsh", None),
        P("wsh", None),
        P("wsh", None),
        P("wsh", None),
        P("wsh"),
        P("wsh", None),
        P("wsh", None),
        P("wsh", None),
        P("wsh", None),
        P("wsh"),
        P("wsh", None),
        P("wsh", None),
        P("wsh", None),
    )
    out_specs = (
        P("wsh", "ctx", None),
        P("wsh", "ctx", None),
        P("wsh", "ctx", None),
        P("wsh"),
        P("wsh", None),
        P("wsh", None),
        P("wsh", None),
        P("wsh", None),
        P("wsh", None),
        P("wsh"),
        P("wsh", None),
        P("wsh", None),
        P("wsh", None),
        P("wsh", None),
        P("wsh"),
        P("wsh", None),
        P("wsh", None),
        P("wsh", None),
    )
    return jax.shard_map(
        on_device, mesh=mesh, in_specs=in_specs, out_specs=out_specs, check_vma=False
    )
```

time: 1570 us -> 860 us (0.55)
  waiting for transfers between devices: 1180 us -> 275 us
  local copies, waits for them, and re-layouts: 74.1 us -> 294 us
  blocking collectives: 100 us -> 0 us
  starting transfers between devices: 1.38 us -> 72.3 us
  other arithmetic: 31.8 us -> 65.3 us
  matrix products: 159 us -> 135 us
    reduce_scatter x11 -> x0, waiting for transfers between devices: 664 us -> none  [the longest x1 77.1 us: on_device(): lax.psum_scatter(down_part.astype(jnp.bfloat16), 'wsh', scatter_dimension...]
    all_gather x13 -> x0, waiting for transfers between devices: 383 us -> none  [the longest x1 59.4 us: on_device(): lax.all_gather(ffn_gate, 'wsh', axis=0, tiled=True)]
    ppermute x0 -> x84, waiting for transfers between devices: none -> 275 us  [exchange(): return lax.ppermute(block, axis, [(i, i ^ bit) for i in range(count)])]
    dynamic_update_slice x0 -> x44, local copies, waits for them, and re-layouts: none -> 154 us  [spread_over(): lax.dynamic_update_slice_in_dim(joined, piece[None], index ^ offset, 0)]
    unnamed x33 -> x0, waiting for transfers between devices: 115 us -> none
    ppermute x0 -> x84, starting transfers between devices: none -> 72.3 us  [exchange(): return lax.ppermute(block, axis, [(i, i ^ bit) for i in range(count)])]
    unnamed x2 -> x0, blocking collectives: 58.8 us -> none
    all_gather x3 -> x0, blocking collectives: 35.6 us -> none  [the longest x1 18.4 us: on_device(): lax.all_gather(bias_table, 'wsh', axis=0, tiled=True)]
  transfers between devices with their start and end apart: 29 -> 84, of which waited for: 25 -> 33; matrix products, arithmetic and copies ran while one was open for 14% -> 44% of each run, Pallas kernels for 0% -> 0%
where the time goes in v1:
time: 860 us; the launch traced here: 846 us
  local copies, waits for them, and re-layouts  294 us (34%)
  waiting for transfers between devices  275 us (32%)
  matrix products  135 us (16%)
  starting transfers between devices  72.3 us (8%)
  other arithmetic  65.3 us (8%)
    ppermute x84, waiting for transfers between devices, exchange(): return lax.ppermute(block, axis, [(i, i ^ bit) for i in range(count)])  275 us
    dynamic_update_slice x44, local copies, waits for them, and re-layouts, spread_over(): lax.dynamic_update_slice_in_dim(joined, piece[None], index ^ offset, 0)  154 us
    ppermute x84, starting transfers between devices, exchange(): return lax.ppermute(block, axis, [(i, i ^ bit) for i in range(count)])  72.3 us
    unnamed x230, local copies, waits for them, and re-layouts  31.7 us
    broadcast_in_dim x14, local copies, waits for them, and re-layouts, spread_over(): piece[None]  25.9 us
    dot_general x14, matrix products, matmul_tn(): lax.dot_general(left_side, right_side, (((0,), (0,)), ((), ())), preferre...  21.4 us
    convert_element_type x21, other arithmetic, reduce_steps(): (kept.astype(jnp.float32) + came.astype(jnp.float32)).astype(jnp.bfloat16)  20.5 us
    dot_general x5, matrix products, score_tile(): jnp.einsum('hqd,khd->hqk', query_heads, key_tile, preferred_element_type=...  17.5 us
  transfers between devices with their start and end apart: 84, of which 33 were waited for; matrix products, arithmetic and copies ran while one was open for 44% of the time, Pallas kernels for 0%

profile of v1, /device:TPU:0, one launch (start us, length us, event | category | flops | bytes accessed | tf_op | source)
XLA Modules:
  0.0 846.0 jit_solution(16398011139047715773)
XLA Ops:
  18.5 8.9 %collective-permute-done = bf16[1,336]{1,0:T(2,128)(2,1)S(1)} collective-permute-done((bf16[1,336]{1,0:T(2,128)(2,1)S(1)}, bf16[1,336]{1,0:T(2,128)(2,1)S(1)}, u32[]{:S(2)}, u32[]{:S(2)}) %collective-permute-start) | collective-permute-done | bytes 704 | tf_op jit(solution)/shard_map/ppermute | solution.py:197
  35.2 28.5 %while.16 = (s32[]{:T(128)}, bf16[2,12,256,512]{2,3,1,0:T(8,128)(2,1)}, s32[256]{0:T(256)S(1)}, s32[2,512]{1,0:T(2,128)S(1)}, bf16[32,12]{0,1:T(8,128)(2,1)S(1)}, /*index=5*/s32[]{:T(128)}) while((s32[]{:T(128)}, bf16[2,12,256,512]{2,3,1,0:T(8,128)(2,1)}, s32[256]{0:T(256)S(1)}, s32[2,512]{1,0:T(2,128)S(1)}, bf16[32,12]{0,1:T(8,128)(2,1)S(1)}, ...), condition=%wide.region_2.3_spmd, body=%wide.region_1.2_spmd.sunk | while | flops 114688000 | bytes 17050452 | solution.py:91
  36.3 5.0 fusion.351
  41.4 6.2 copy.234
  50.5 5.0 fusion.351
  55.5 6.2 copy.234
  75.0 4.3 collective-permute-done.16
  81.4 4.2 collective-permute-done.4
  100.7 9.7 %collective-permute-done.5 = bf16[4,96,768]{2,1,0:T(8,128)(2,1)S(1)} collective-permute-done((bf16[4,96,768]{2,1,0:T(8,128)(2,1)S(1)}, bf16[4,96,768]{2,1,0:T(8,128)(2,1)S(1)}, u32[]{:S(2)}, u32[]{:S(2)}) %collective-permute-start.5) | collective-permute-done | bytes 589856 | tf_op jit(solution)/shard_map/ppermute | solution.py:197
  111.5 10.3 %collective-permute-done.29 = bf16[4,96,1024]{2,1,0:T(8,128)(2,1)S(1)} collective-permute-done((bf16[4,96,1024]{2,1,0:T(8,128)(2,1)S(1)}, bf16[4,96,1024]{2,1,0:T(8,128)(2,1)S(1)}, u32[]{:S(2)}, u32[]{:S(2)}) %collective-permute-start.29) | collective-permute-done | bytes 786464 | tf_op jit(solution)/shard_map/ppermute | solution.py:197
  125.6 12.0 %collective-permute-done.18 = bf16[8,96,768]{2,1,0:T(8,128)(2,1)S(1)} collective-permute-done((bf16[8,96,768]{2,1,0:T(8,128)(2,1)S(1)}, bf16[8,96,768]{2,1,0:T(8,128)(2,1)S(1)}, u32[]{:S(2)}, u32[]{:S(2)}) %collective-permute-start.18) | collective-permute-done | bytes 1179680 | tf_op jit(solution)/shard_map/ppermute | solution.py:197
  138.4 24.5 %collective-permute-done.6 = bf16[8,96,768]{2,1,0:T(8,128)(2,1)S(1)} collective-permute-done((bf16[8,96,768]{2,1,0:T(8,128)(2,1)S(1)}, bf16[8,96,768]{2,1,0:T(8,128)(2,1)S(1)}, u32[]{:S(2)}, u32[]{:S(2)}) %collective-permute-start.6) | collective-permute-done | bytes 1179680 | tf_op jit(solution)/shard_map/ppermute | solution.py:197
  168.0 22.8 %collective-permute-done.30 = bf16[8,96,1024]{2,1,0:T(8,128)(2,1)S(1)} collective-permute-done((bf16[8,96,1024]{2,1,0:T(8,128)(2,1)S(1)}, bf16[8,96,1024]{2,1,0:T(8,128)(2,1)S(1)}, u32[]{:S(2)}, u32[]{:S(2)}) %collective-permute-start.30) | collective-permute-done | bytes 1572896 | tf_op jit(solution)/shard_map/ppermute | solution.py:197
  216.6 16.7 %dynamic_update_slice.164 = bf16[4,256,768]{1,0,2:T(4,128)(2,1)} dynamic-update-slice(bf16[4,256,768]{1,0,2:T(4,128)(2,1)} %broadcast.493.clone, bf16[1,256,768]{1,0,2:T(2,128)(2,1)S(1)} %copy-done.75, s32[]{:T(128)S(6)} %select_n.382, s32[]{:T(128)} %constant.361.clone.1, s32[]{:T(128)} %constant.361.clone.1) | dynamic-update-slice | bytes 786436 | tf_op jit(solution)/shard_map/dynamic_update_slice | solution.py:226
  234.8 16.3 %dynamic_update_slice.168 = bf16[4,256,768]{1,0,2:T(4,128)(2,1)} dynamic-update-slice(bf16[4,256,768]{1,0,2:T(4,128)(2,1)} %broadcast.493.clone.1, bf16[1,256,768]{1,0,2:T(2,128)(2,1)S(1)} %copy-done.76, s32[]{:T(128)S(6)} %select_n.382, s32[]{:T(128)} %constant.361.clone.1, s32[]{:T(128)} %constant.361.clone.1) | dynamic-update-slice | bytes 786436 | tf_op jit(solution)/shard_map/dynamic_update_slice | solution.py:226
  255.3 8.3 dynamic_update_slice.178
  283.3 10.4 %dynamic_update_slice.179 = bf16[4,128,768]{1,0,2:T(4,128)(2,1)} dynamic-update-slice(bf16[4,128,768]{1,0,2:T(4,128)(2,1)} %copy-done.74, bf16[1,128,768]{1,0,2:T(2,128)(2,1)} %copy.153, s32[]{:T(128)S(6)} %select_n.385, s32[]{:T(128)} %constant.361.clone.1, s32[]{:T(128)} %constant.361.clone.1) | dynamic-update-slice | bytes 393220 | tf_op jit(solution)/shard_map/dynamic_update_slice | solution.py:226
  296.1 10.0 %dynamic_update_slice.165 = bf16[4,256,768]{1,0,2:T(4,128)(2,1)S(1)} dynamic-update-slice(bf16[4,256,768]{1,0,2:T(4,128)(2,1)S(1)} %copy-done.49, bf16[1,256,768]{1,0,2:T(2,128)(2,1)S(1)} %copy.133, s32[]{:T(128)S(6)} %select_n.383, s32[]{:T(128)} %constant.361.clone.1, s32[]{:T(128)} %constant.361.clone.1) | dynamic-update-slice | bytes 786436 | tf_op jit(solution)/shard_map/dynamic_update_slice | solution.py:226
  306.2 14.4 %dynamic_update_slice.166 = bf16[4,256,768]{1,0,2:T(4,128)(2,1)S(1)} dynamic-update-slice(bf16[4,256,768]{1,0,2:T(4,128)(2,1)S(1)} %dynamic_update_slice.165, bf16[1,256,768]{1,0,2:T(2,128)(2,1)} %copy.134, s32[]{:T(128)S(6)} %select_n.384, s32[]{:T(128)} %constant.361.clone.1, s32[]{:T(128)} %constant.361.clone.1) | dynamic-update-slice | bytes 786436 | tf_op jit(solution)/shard_map/dynamic_update_slice | solution.py:226
  320.6 16.3 %dynamic_update_slice.169 = bf16[4,256,768]{1,0,2:T(4,128)(2,1)} dynamic-update-slice(bf16[4,256,768]{1,0,2:T(4,128)(2,1)} %dynamic_update_slice.168, bf16[1,256,768]{1,0,2:T(2,128)(2,1)S(1)} %copy-done.73, s32[]{:T(128)S(6)} %select_n.383, s32[]{:T(128)} %constant.361.clone.1, s32[]{:T(128)} %constant.361.clone.1) | dynamic-update-slice | bytes 786436 | tf_op jit(solution)/shard_map/dynamic_update_slice | solution.py:226
  336.9 16.3 %dynamic_update_slice.170 = bf16[4,256,768]{1,0,2:T(4,128)(2,1)} dynamic-update-slice(bf16[4,256,768]{1,0,2:T(4,128)(2,1)} %dynamic_update_slice.169, bf16[1,256,768]{1,0,2:T(2,128)(2,1)} %copy.142, s32[]{:T(128)S(6)} %select_n.384, s32[]{:T(128)} %constant.361.clone.1, s32[]{:T(128)} %constant.361.clone.1) | dynamic-update-slice | bytes 786436 | tf_op jit(solution)/shard_map/dynamic_update_slice | solution.py:226
  355.8 10.0 %dynamic_update_slice.167 = bf16[4,256,768]{1,0,2:T(4,128)(2,1)S(1)} dynamic-update-slice(bf16[4,256,768]{1,0,2:T(4,128)(2,1)S(1)} %dynamic_update_slice.166, bf16[1,256,768]{1,0,2:T(2,128)(2,1)S(1)} %copy.135, s32[]{:T(128)S(6)} %select_n.385, s32[]{:T(128)} %constant.361.clone.1, s32[]{:T(128)} %constant.361.clone.1) | dynamic-update-slice | bytes 786436 | tf_op jit(solution)/shard_map/dynamic_update_slice | solution.py:226
  369.9 21.4 %while.17 = (s32[]{:T(128)}, f32[12,256]{1,0:T(8,128)S(1)}, f32[12,256]{1,0:T(8,128)S(1)}, bf16[2,512,12,64]{1,3,2,0:T(8,128)(2,1)S(1)}, bf16[12,256,64]{1,2,0:T...) while((s32[]{:T(128)}, f32[12,256]{1,0:T(8,128)S(1)}, ...), condition=%wide.region_6.7_spmd.clone, body=%wide.region_3.6_spmd.clone.sunk | while | flops 212352000 | bytes 20214892 | solution.py:114
  369.9 5.7 fusion.353
  375.6 5.0 exponential_reduce_fusion.3
  380.6 5.7 fusion.353
  386.3 5.0 exponential_reduce_fusion.3
  393.5 16.5 %dynamic_update_slice.171 = bf16[4,256,768]{1,0,2:T(4,128)(2,1)} dynamic-update-slice(bf16[4,256,768]{1,0,2:T(4,128)(2,1)} %dynamic_update_slice.170, bf16[1,256,768]{1,0,2:T(2,128)(2,1)S(1)} %copy.143, s32[]{:T(128)S(6)} %select_n.385, s32[]{:T(128)} %constant.361.clone.1, s32[]{:T(128)} %constant.361.clone.1) | dynamic-update-slice | bytes 786436 | tf_op jit(solution)/shard_map/dynamic_update_slice | solution.py:226
  410.0 4.7 reshape.614
  417.7 8.6 %while.18 = (s32[]{:T(128)}, f32[12,256,64]{1,2,0:T(8,128)S(1)}, bf16[2,512,12,64]{1,3,2,0:T(8,128)(2,1)S(1)}, bf16[12,256,64]{1,2,0:T(8,128)(2,1)S(1)}, bf16[2,...) while((s32[]{:T(128)}, f32[12,256,64]{1,2,0:T(8,128)S(1)}, ...), condition=%wide.region_8.9_spmd.clone, body=%wide.region_7.8_spmd.clone.sunk | while | flops 409337856 | bytes 6703214 | solution.py:126
  417.7 4.3 fusion.359
  421.9 4.3 fusion.359
  456.2 5.2 fusion.121
  489.7 43.1 %while.19 = (s32[]{:T(128)}, f32[12,256,64]{1,2,0:T(8,128)}, f32[32,12]{0,1:T(8,128)S(1)}, bf16[2,512,12,64]{1,3,2,0:T(8,128)(2,1)}, bf16[2,512,12,64]{1,3,2,0:T...) while((s32[]{:T(128)}, f32[12,256,64]{1,2,0:T(8,128)}, ...), condition=%wide.region_18.19_spmd.clone, body=%wide.region_17.18_spmd.clone.sunk | while | flops 1134035712 | bytes 167039568 | solution.py:181
  598.2 8.3 collective-permute-done.40
  608.4 5.4 collective-permute-done.42
  623.8 6.3 collective-permute-start.49
  640.0 13.1 %collective-permute-done.77 = bf16[2,2,2,64,768]{4,3,2,1,0:T(8,128)(2,1)S(1)} collective-permute-done((bf16[2,2,2,64,768]{4,3,2,1,0:T(8,128)(2,1)S(1)}, bf16[2,2,2,64,768]{4,3,2,1,0:T(8,128)(2,1)S(1)}, u32[]{:S(2)}, u32[]{:S(2)}) %collective-permute-start.77) | collective-permute-done | bytes 786464 | tf_op jit(solution)/shard_map/ppermute | solution.py:197
  655.1 8.7 %collective-permute-done.78 = bf16[2,2,64,768]{3,2,1,0:T(8,128)(2,1)S(1)} collective-permute-done((bf16[2,2,64,768]{3,2,1,0:T(8,128)(2,1)S(1)}, bf16[2,2,64,768]{3,2,1,0:T(8,128)(2,1)S(1)}, u32[]{:S(2)}, u32[]{:S(2)}) %collective-permute-start.78) | collective-permute-done | bytes 393248 | tf_op jit(solution)/shard_map/ppermute | solution.py:197
  681.2 4.4 fusion.92
  685.6 13.9 %collective-permute-done.61 = bf16[2,2,2,96,768]{4,3,1,2,0:T(8,128)(2,1)} collective-permute-done((bf16[2,2,2,96,768]{4,3,1,2,0:T(8,128)(2,1)}, bf16[2,2,2,96,768]{4,3,1,2,0:T(8,128)(2,1)}, u32[]{:S(2)}, u32[]{:S(2)}) %collective-permute-start.61) | collective-permute-done | bytes 1179680 | tf_op jit(solution)/shard_map/ppermute | solution.py:197
  706.4 11.0 %collective-permute-done.62 = bf16[2,2,96,768]{3,2,0,1:T(8,128)(2,1)S(1)} collective-permute-done((bf16[2,2,96,768]{3,2,0,1:T(8,128)(2,1)S(1)}, bf16[2,2,96,768]{3,2,0,1:T(8,128)(2,1)S(1)}, u32[]{:S(2)}, u32[]{:S(2)}) %collective-permute-start.62) | collective-permute-done | bytes 589856 | tf_op jit(solution)/shard_map/ppermute | solution.py:197
  719.6 4.9 collective-permute-done.63
  726.6 46.3 %collective-permute-done.53 = bf16[2,2,2,96,768]{4,3,0,1,2:T(8,128)(2,1)S(1)} collective-permute-done((bf16[2,2,2,96,768]{4,3,0,1,2:T(8,128)(2,1)S(1)}, bf16[2,2,2,96,768]{4,3,0,1,2:T(8,128)(2,1)S(1)}, u32[]{:S(2)}, u32[]{:S(2)}) %collective-permute-start.53) | collective-permute-done | bytes 1179680 | tf_op jit(solution)/shard_map/ppermute | solution.py:197
  778.6 10.9 %collective-permute-done.54 = bf16[2,2,96,768]{3,2,0,1:T(8,128)(2,1)S(1)} collective-permute-done((bf16[2,2,96,768]{3,2,0,1:T(8,128)(2,1)S(1)}, bf16[2,2,96,768]{3,2,0,1:T(8,128)(2,1)S(1)}, u32[]{:S(2)}, u32[]{:S(2)}) %collective-permute-start.54) | collective-permute-done | bytes 589856 | tf_op jit(solution)/shard_map/ppermute | solution.py:197
  790.9 5.6 collective-permute-done.55
  811.8 11.0 %collective-permute-done.72 = bf16[96,1024]{1,0:T(8,128)(2,1)S(1)} collective-permute-done((bf16[96,1024]{1,0:T(8,128)(2,1)S(1)}, bf16[96,1024]{1,0:T(8,128)(2,1)S(1)}, u32[]{:S(2)}, u32[]{:S(2)}) %collective-permute-start.72) | collective-permute-done | bytes 196640 | tf_op jit(solution)/shard_map/ppermute | solution.py:197
  823.6 5.9 collective-permute-done.73
  (761 shorter events, 391.5 us)
Async XLA Ops:
  2.6 62.6 %collective-permute-start.15 = (bf16[1,96,768]{2,1,0:T(8,128)(2,1)}, bf16[1,96,768]{2,1,0:T(8,128)(2,1)}, u32[]{:S(2)}, u32[]{:S(2)}) collective-permute-start(bf16[1,96,768]{2,1,0:T(8,128)(2,1)} %fusion.196), channel_id=1, source_target_pairs={{0,4},{1,5},{2,6},{3,7},{4,0},{5,1},{6,2},{7,3},{8,12},{9,13},{10,... | collective-permute-start | bytes 442376 | tf_op jit(solution)/shard_map/ppermute | solution.py:197
  7.7 60.6 %collective-permute-start.3 = (bf16[1,96,768]{2,1,0:T(8,128)(2,1)S(1)}, bf16[1,96,768]{2,1,0:T(8,128)(2,1)}, u32[]{:S(2)}, u32[]{:S(2)}) collective-permute-start(bf16[1,96,768]{2,1,0:T(8,128)(2,1)S(1)} %fusion.200), channel_id=1, source_target_pairs={{0,4},{1,5},{2,6},{3,7},{4,0},{5,1},{6,2},{7,3},{8,12},{9,13},{10,... | collective-permute-start | bytes 442376 | tf_op jit(solution)/shard_map/ppermute | solution.py:197
  9.3 18.1 %collective-permute-start = (bf16[1,336]{1,0:T(2,128)(2,1)S(1)}, bf16[1,336]{1,0:T(2,128)(2,1)S(1)}, u32[]{:S(2)}, u32[]{:S(2)}) collective-permute-start(bf16[1,336]{1,0:T(2,128)(2,1)S(1)} %broadcast_in_dim.236), channel_id=1, source_target_pairs={{0,4},{1,5},{2,6},{3,7},{4,0},{5,1},{6,2},{7,3},{8,12},{9,13},{10,... | collective-permute-start | bytes 2024 | tf_op jit(solution)/shard_map/ppermute | solution.py:197
  13.8 50.3 %collective-permute-start.33 = (bf16[1,64,768]{2,1,0:T(8,128)(2,1)}, bf16[1,64,768]{2,1,0:T(8,128)(2,1)}, u32[]{:S(2)}, u32[]{:S(2)}) collective-permute-start(bf16[1,64,768]{2,1,0:T(8,128)(2,1)} %dynamic-slice_bitcast_fusion.21), channel_id=1, source_target_pairs={{0,4},{1,5},{2,6},{3,7},{4,0},{5,1},{6,2},{7,3},{8,12},{9,13},{10,... | collective-permute-start | bytes 294920 | tf_op jit(solution)/shard_map/ppermute | solution.py:197
  14.6 54.8 %collective-permute-start.27 = (bf16[1,96,1024]{2,1,0:T(8,128)(2,1)}, bf16[1,96,1024]{2,1,0:T(8,128)(2,1)}, u32[]{:S(2)}, u32[]{:S(2)}) collective-permute-start(bf16[1,96,1024]{2,1,0:T(8,128)(2,1)} %fusion.183), channel_id=1, source_target_pairs={{0,4},{1,5},{2,6},{3,7},{4,0},{5,1},{6,2},{7,3},{8,12},{9,13},{10,... | collective-permute-start | bytes 589832 | tf_op jit(solution)/shard_map/ppermute | solution.py:197
  69.3 16.4 %collective-permute-start.4 = (bf16[2,96,768]{2,1,0:T(8,128)(2,1)S(1)}, bf16[2,96,768]{2,1,0:T(8,128)(2,1)S(1)}, u32[]{:S(2)}, u32[]{:S(2)}) collective-permute-start(bf16[2,96,768]{2,1,0:T(8,128)(2,1)S(1)} %maximum_bitcast_fusion.1), channel_id=1, source_target_pairs={{0,2},{1,3},{2,0},{3,1},{4,6},{5,7},{6,4},{7,5},{8,10},{9,11},{10,... | collective-permute-start | bytes 884744 | tf_op jit(solution)/shard_map/ppermute | solution.py:197
  70.5 19.6 %collective-permute-start.28 = (bf16[2,96,1024]{2,1,0:T(8,128)(2,1)S(1)}, bf16[2,96,1024]{2,1,0:T(8,128)(2,1)S(1)}, u32[]{:S(2)}, u32[]{:S(2)}) collective-permute-start(bf16[2,96,1024]{2,1,0:T(8,128)(2,1)S(1)} %maximum_bitcast_fusion), channel_id=1, source_target_pairs={{0,2},{1,3},{2,0},{3,1},{4,6},{5,7},{6,4},{7,5},{8,10},{9,11},{10,... | collective-permute-start | bytes 1179656 | tf_op jit(solution)/shard_map/ppermute | solution.py:197
  73.1 18.5 %collective-permute-start.35 = (bf16[4,64,768]{2,1,0:T(8,128)(2,1)S(1)}, bf16[4,64,768]{2,1,0:T(8,128)(2,1)S(1)}, u32[]{:S(2)}, u32[]{:S(2)}) collective-permute-start(bf16[4,64,768]{2,1,0:T(8,128)(2,1)S(1)} %bitcast.904), channel_id=1, source_target_pairs={{0,1},{1,0},{2,3},{3,2},{4,5},{5,4},{6,7},{7,6},{8,9},{9,8},{10,11... | collective-permute-start | bytes 1179656 | tf_op jit(solution)/shard_map/ppermute | solution.py:197
  79.5 18.4 %collective-permute-start.17 = (bf16[4,96,768]{2,1,0:T(8,128)(2,1)S(1)}, bf16[4,96,768]{2,1,0:T(8,128)(2,1)S(1)}, u32[]{:S(2)}, u32[]{:S(2)}) collective-permute-start(bf16[4,96,768]{2,1,0:T(8,128)(2,1)S(1)} %bitcast.903), channel_id=1, source_target_pairs={{0,1},{1,0},{2,3},{3,2},{4,5},{5,4},{6,7},{7,6},{8,9},{9,8},{10,11... | collective-permute-start | bytes 1769480 | tf_op jit(solution)/shard_map/ppermute | solution.py:197
  85.7 24.7 %collective-permute-start.5 = (bf16[4,96,768]{2,1,0:T(8,128)(2,1)S(1)}, bf16[4,96,768]{2,1,0:T(8,128)(2,1)S(1)}, u32[]{:S(2)}, u32[]{:S(2)}) collective-permute-start(bf16[4,96,768]{2,1,0:T(8,128)(2,1)S(1)} %bitcast.902), channel_id=1, source_target_pairs={{0,1},{1,0},{2,3},{3,2},{4,5},{5,4},{6,7},{7,6},{8,9},{9,8},{10,11... | collective-permute-start | bytes 1769480 | tf_op jit(solution)/shard_map/ppermute | solution.py:197
  90.2 31.6 %collective-permute-start.29 = (bf16[4,96,1024]{2,1,0:T(8,128)(2,1)S(1)}, bf16[4,96,1024]{2,1,0:T(8,128)(2,1)S(1)}, u32[]{:S(2)}, u32[]{:S(2)}) collective-permute-start(bf16[4,96,1024]{2,1,0:T(8,128)(2,1)S(1)} %bitcast.901), channel_id=1, source_target_pairs={{0,1},{1,0},{2,3},{3,2},{4,5},{5,4},{6,7},{7,6},{8,9},{9,8},{10,11... | collective-permute-start | bytes 2359304 | tf_op jit(solution)/shard_map/ppermute | solution.py:197
  91.8 32.8 %collective-permute-start.36 = (bf16[8,64,768]{2,1,0:T(8,128)(2,1)S(1)}, bf16[8,64,768]{2,1,0:T(8,128)(2,1)S(1)}, u32[]{:S(2)}, u32[]{:S(2)}) collective-permute-start(bf16[8,64,768]{2,1,0:T(8,128)(2,1)S(1)} %bitcast.898), channel_id=1, source_target_pairs={{0,16},{8,24},{16,0},{24,8},{1,17},{9,25},{17,1},{25,9},{2,18},{10... | collective-permute-start | bytes 2359304 | tf_op jit(solution)/shard_map/ppermute | solution.py:197
  93.4 31.4 %collective-permute-start.37 = (bf16[8,64,768]{2,1,0:T(8,128)(2,1)S(1)}, bf16[8,64,768]{2,1,0:T(8,128)(2,1)S(1)}, u32[]{:S(2)}, u32[]{:S(2)}) collective-permute-start(bf16[8,64,768]{2,1,0:T(8,128)(2,1)S(1)} %bitcast.899), channel_id=1, source_target_pairs={{0,8},{8,0},{16,24},{24,16},{1,9},{9,1},{17,25},{25,17},{2,10},{10... | collective-permute-start | bytes 2359304 | tf_op jit(solution)/shard_map/ppermute | solution.py:197
  98.2 39.4 %collective-permute-start.18 = (bf16[8,96,768]{2,1,0:T(8,128)(2,1)S(1)}, bf16[8,96,768]{2,1,0:T(8,128)(2,1)S(1)}, u32[]{:S(2)}, u32[]{:S(2)}) collective-permute-start(bf16[8,96,768]{2,1,0:T(8,128)(2,1)S(1)} %bitcast.882), channel_id=1, source_target_pairs={{0,16},{8,24},{16,0},{24,8},{1,17},{9,25},{17,1},{25,9},{2,18},{10... | collective-permute-start | bytes 3538952 | tf_op jit(solution)/shard_map/ppermute | solution.py:197
  110.5 27.3 %collective-permute-start.19 = (bf16[8,96,768]{2,1,0:T(8,128)(2,1)S(1)}, bf16[8,96,768]{2,1,0:T(8,128)(2,1)S(1)}, u32[]{:S(2)}, u32[]{:S(2)}) collective-permute-start(bf16[8,96,768]{2,1,0:T(8,128)(2,1)S(1)} %bitcast.884), channel_id=1, source_target_pairs={{0,8},{8,0},{16,24},{24,16},{1,9},{9,1},{17,25},{25,17},{2,10},{10... | collective-permute-start | bytes 3538952 | tf_op jit(solution)/shard_map/ppermute | solution.py:197
  121.8 41.1 %collective-permute-start.6 = (bf16[8,96,768]{2,1,0:T(8,128)(2,1)S(1)}, bf16[8,96,768]{2,1,0:T(8,128)(2,1)S(1)}, u32[]{:S(2)}, u32[]{:S(2)}) collective-permute-start(bf16[8,96,768]{2,1,0:T(8,128)(2,1)S(1)} %bitcast.886), channel_id=1, source_target_pairs={{0,16},{8,24},{16,0},{24,8},{1,17},{9,25},{17,1},{25,9},{2,18},{10... | collective-permute-start | bytes 3538952 | tf_op jit(solution)/shard_map/ppermute | solution.py:197
  124.5 38.5 %collective-permute-start.7 = (bf16[8,96,768]{2,1,0:T(8,128)(2,1)S(1)}, bf16[8,96,768]{2,1,0:T(8,128)(2,1)S(1)}, u32[]{:S(2)}, u32[]{:S(2)}) collective-permute-start(bf16[8,96,768]{2,1,0:T(8,128)(2,1)S(1)} %bitcast.887), channel_id=1, source_target_pairs={{0,8},{8,0},{16,24},{24,16},{1,9},{9,1},{17,25},{25,17},{2,10},{10... | collective-permute-start | bytes 3538952 | tf_op jit(solution)/shard_map/ppermute | solution.py:197
  124.7 66.1 %collective-permute-start.30 = (bf16[8,96,1024]{2,1,0:T(8,128)(2,1)S(1)}, bf16[8,96,1024]{2,1,0:T(8,128)(2,1)S(1)}, u32[]{:S(2)}, u32[]{:S(2)}) collective-permute-start(bf16[8,96,1024]{2,1,0:T(8,128)(2,1)S(1)} %bitcast.874), channel_id=1, source_target_pairs={{0,16},{8,24},{16,0},{24,8},{1,17},{9,25},{17,1},{25,9},{2,18},{10... | collective-permute-start | bytes 4718600 | tf_op jit(solution)/shard_map/ppermute | solution.py:197
  137.6 54.4 %collective-permute-start.31 = (bf16[8,96,1024]{2,1,0:T(8,128)(2,1)S(1)}, bf16[8,96,1024]{2,1,0:T(8,128)(2,1)S(1)}, u32[]{:S(2)}, u32[]{:S(2)}) collective-permute-start(bf16[8,96,1024]{2,1,0:T(8,128)(2,1)S(1)} %bitcast.875), channel_id=1, source_target_pairs={{0,8},{8,0},{16,24},{24,16},{1,9},{9,1},{17,25},{25,17},{2,10},{10... | collective-permute-start | bytes 4718600 | tf_op jit(solution)/shard_map/ppermute | solution.py:197
  137.7 26.0 %collective-permute-start.38 = (bf16[8,64,768]{2,1,0:T(8,128)(2,1)S(1)}, bf16[8,64,768]{2,1,0:T(8,128)(2,1)S(1)}, u32[]{:S(2)}, u32[]{:S(2)}) collective-permute-start(bf16[8,64,768]{2,1,0:T(8,128)(2,1)S(1)} %collective-permute-done.36), channel_id=1, source_target_pairs={{0,8},{8,0},{16,24},{24,16},{1,9},{9,1},{17,25},{25,17},{2,10},{10... | collective-permute-start | bytes 2359304 | tf_op jit(solution)/shard_map/ppermute | solution.py:197
  162.9 29.3 %collective-permute-start.20 = (bf16[8,96,768]{2,1,0:T(8,128)(2,1)S(1)}, bf16[8,96,768]{2,1,0:T(8,128)(2,1)S(1)}, u32[]{:S(2)}, u32[]{:S(2)}) collective-permute-start(bf16[8,96,768]{2,1,0:T(8,128)(2,1)S(1)} %collective-permute-done.18), channel_id=1, source_target_pairs={{0,8},{8,0},{16,24},{24,16},{1,9},{9,1},{17,25},{25,17},{2,10},{10... | collective-permute-start | bytes 3538952 | tf_op jit(solution)/shard_map/ppermute | solution.py:197
  163.0 29.2 %collective-permute-start.8 = (bf16[8,96,768]{2,1,0:T(8,128)(2,1)S(1)}, bf16[8,96,768]{2,1,0:T(8,128)(2,1)S(1)}, u32[]{:S(2)}, u32[]{:S(2)}) collective-permute-start(bf16[8,96,768]{2,1,0:T(8,128)(2,1)S(1)} %collective-permute-done.6), channel_id=1, source_target_pairs={{0,8},{8,0},{16,24},{24,16},{1,9},{9,1},{17,25},{25,17},{2,10},{10... | collective-permute-start | bytes 3538952 | tf_op jit(solution)/shard_map/ppermute | solution.py:197
  197.1 68.7 %collective-permute-start.9 = (bf16[256,768]{1,0:T(8,128)(2,1)}, bf16[256,768]{1,0:T(8,128)(2,1)}, u32[]{:S(2)}, u32[]{:S(2)}) collective-permute-start(bf16[256,768]{1,0:T(8,128)(2,1)} %convolution_convert_fusion.22), channel_id=1, source_target_pairs={{0,16},{8,24},{16,0},{24,8},{1,17},{9,25},{17,1},{25,9},{2,18},{10... | collective-permute-start | bytes 1179656 | tf_op jit(solution)/shard_map/ppermute | solution.py:197
  198.5 70.4 %collective-permute-start.10 = (bf16[256,768]{1,0:T(8,128)(2,1)}, bf16[256,768]{1,0:T(8,128)(2,1)}, u32[]{:S(2)}, u32[]{:S(2)}) collective-permute-start(bf16[256,768]{1,0:T(8,128)(2,1)} %convolution_convert_fusion.22), channel_id=1, source_target_pairs={{0,8},{8,0},{16,24},{24,16},{1,9},{9,1},{17,25},{25,17},{2,10},{10... | collective-permute-start | bytes 1179656 | tf_op jit(solution)/shard_map/ppermute | solution.py:197
  203.5 48.3 %collective-permute-start.21 = (bf16[128,768]{0,1:T(8,128)(2,1)}, bf16[128,768]{0,1:T(8,128)(2,1)}, u32[]{:S(2)}, u32[]{:S(2)}) collective-permute-start(bf16[128,768]{0,1:T(8,128)(2,1)} %bitcast.67), channel_id=1, source_target_pairs={{0,16},{8,24},{16,0},{24,8},{1,17},{9,25},{17,1},{25,9},{2,18},{10... | collective-permute-start | bytes 589832 | tf_op jit(solution)/shard_map/ppermute | solution.py:197
  204.1 49.9 %collective-permute-start.22 = (bf16[128,768]{0,1:T(8,128)(2,1)}, bf16[128,768]{0,1:T(8,128)(2,1)}, u32[]{:S(2)}, u32[]{:S(2)}) collective-permute-start(bf16[128,768]{0,1:T(8,128)(2,1)} %bitcast.67), channel_id=1, source_target_pairs={{0,8},{8,0},{16,24},{24,16},{1,9},{9,1},{17,25},{25,17},{2,10},{10... | collective-permute-start | bytes 589832 | tf_op jit(solution)/shard_map/ppermute | solution.py:197
  210.5 61.9 %collective-permute-start.12 = (bf16[256,768]{1,0:T(8,128)(2,1)}, bf16[256,768]{1,0:T(8,128)(2,1)}, u32[]{:S(2)}, u32[]{:S(2)}) collective-permute-start(bf16[256,768]{1,0:T(8,128)(2,1)} %convolution_convert_fusion.20), channel_id=1, source_target_pairs={{0,16},{8,24},{16,0},{24,8},{1,17},{9,25},{17,1},{25,9},{2,18},{10... | collective-permute-start | bytes 1179656 | tf_op jit(solution)/shard_map/ppermute | solution.py:197
  254.0 21.5 %collective-permute-start.13 = (bf16[256,768]{1,0:T(8,128)(2,1)}, bf16[256,768]{1,0:T(8,128)(2,1)}, u32[]{:S(2)}, u32[]{:S(2)}) collective-permute-start(bf16[256,768]{1,0:T(8,128)(2,1)} %convolution_convert_fusion.20), channel_id=1, source_target_pairs={{0,8},{8,0},{16,24},{24,16},{1,9},{9,1},{17,25},{25,17},{2,10},{10... | collective-permute-start | bytes 1179656 | tf_op jit(solution)/shard_map/ppermute | solution.py:197
  265.7 87.9 %collective-permute-start.11 = (bf16[256,768]{1,0:T(8,128)(2,1)}, bf16[256,768]{1,0:T(8,128)(2,1)}, u32[]{:S(2)}, u32[]{:S(2)}) collective-permute-start(bf16[256,768]{1,0:T(8,128)(2,1)} %collective-permute-done.9), channel_id=1, source_target_pairs={{0,8},{8,0},{16,24},{24,16},{1,9},{9,1},{17,25},{25,17},{2,10},{10... | collective-permute-start | bytes 1179656 | tf_op jit(solution)/shard_map/ppermute | solution.py:197
  269.0 169.4 %collective-permute-start.32 = (bf16[8,96,1024]{2,1,0:T(8,128)(2,1)}, bf16[8,96,1024]{2,1,0:T(8,128)(2,1)}, u32[]{:S(2)}, u32[]{:S(2)}) collective-permute-start(bf16[8,96,1024]{2,1,0:T(8,128)(2,1)} %copy-done.101), channel_id=1, source_target_pairs={{0,8},{8,0},{16,24},{24,16},{1,9},{9,1},{17,25},{25,17},{2,10},{10... | collective-permute-start | bytes 4718600 | tf_op jit(solution)/shard_map/ppermute | solution.py:197
  353.2 38.1 %collective-permute-start.14 = (bf16[256,768]{1,0:T(8,128)(2,1)}, bf16[256,768]{1,0:T(8,128)(2,1)}, u32[]{:S(2)}, u32[]{:S(2)}) collective-permute-start(bf16[256,768]{1,0:T(8,128)(2,1)} %collective-permute-done.12), channel_id=1, source_target_pairs={{0,8},{8,0},{16,24},{24,16},{1,9},{9,1},{17,25},{25,17},{2,10},{10... | collective-permute-start | bytes 1179656 | tf_op jit(solution)/shard_map/ppermute | solution.py:197
  540.4 52.5 %collective-permute-start.39 = (bf16[2,256,768]{1,2,0:T(8,128)(2,1)}, bf16[2,256,768]{1,2,0:T(8,128)(2,1)}, u32[]{:S(2)}, u32[]{:S(2)}) collective-permute-start(bf16[2,256,768]{1,2,0:T(8,128)(2,1)} %bitcast.758), channel_id=1, source_target_pairs={{0,8},{8,0},{16,24},{24,16},{1,9},{9,1},{17,25},{25,17},{2,10},{10... | collective-permute-start | bytes 2359304 | tf_op jit(solution)/shard_map/ppermute | solution.py:197
  548.1 47.9 %collective-permute-start.41 = (bf16[2,256,768]{1,2,0:T(8,128)(2,1)}, bf16[2,256,768]{1,2,0:T(8,128)(2,1)}, u32[]{:S(2)}, u32[]{:S(2)}) collective-permute-start(bf16[2,256,768]{1,2,0:T(8,128)(2,1)} %bitcast.757), channel_id=1, source_target_pairs={{0,8},{8,0},{16,24},{24,16},{1,9},{9,1},{17,25},{25,17},{2,10},{10... | collective-permute-start | bytes 2359304 | tf_op jit(solution)/shard_map/ppermute | solution.py:197
  552.7 17.6 %collective-permute-start.45 = (bf16[2,128,768]{2,1,0:T(8,128)(2,1)}, bf16[2,128,768]{2,1,0:T(8,128)(2,1)}, u32[]{:S(2)}, u32[]{:S(2)}) collective-permute-start(bf16[2,128,768]{2,1,0:T(8,128)(2,1)} %bitcast.153), channel_id=1, source_target_pairs={{0,8},{8,0},{16,24},{24,16},{1,9},{9,1},{17,25},{25,17},{2,10},{10... | collective-permute-start | bytes 1179656 | tf_op jit(solution)/shard_map/ppermute | solution.py:197
  570.0 111.2 %collective-permute-start.68 = (bf16[2,2,2,2,96,1024]{5,4,3,2,1,0:T(8,128)(2,1)}, bf16[2,2,2,2,96,1024]{5,4,3,2,1,0:T(8,128)(2,1)}, u32[]{:S(2)}, u32[]{:S(2)}) collective-permute-start(bf16[2,2,2,2,96,1024]{5,4,3,2,1,0:T(8,128)(2,1)} %dynamic-slice_bitcast_fusion), channel_id=1, source_target_pairs={{0,8},{8,0},{16,24},{24,16},{1,9},{9,1},{17,25},{25,17},{2,10},{10... | collective-permute-start | bytes 9437192 | tf_op jit(solution)/shard_map/ppermute | solution.py:197
  581.1 49.0 %collective-permute-start.76 = (bf16[2,2,2,2,64,768]{5,4,3,2,1,0:T(8,128)(2,1)}, bf16[2,2,2,2,64,768]{5,4,3,2,1,0:T(8,128)(2,1)}, u32[]{:S(2)}, u32[]{:S(2)}) collective-permute-start(bf16[2,2,2,2,64,768]{5,4,3,2,1,0:T(8,128)(2,1)} %fusion.101), channel_id=1, source_target_pairs={{0,8},{8,0},{16,24},{24,16},{1,9},{9,1},{17,25},{25,17},{2,10},{10... | collective-permute-start | bytes 4718600 | tf_op jit(solution)/shard_map/ppermute | solution.py:197
  589.2 81.2 %collective-permute-start.60 = (bf16[2,2,2,2,96,768]{5,4,1,2,0,3:T(8,128)(2,1)}, bf16[2,2,2,2,96,768]{5,4,1,2,0,3:T(8,128)(2,1)}, u32[]{:S(2)}, u32[]{:S(2)}) collective-permute-start(bf16[2,2,2,2,96,768]{5,4,1,2,0,3:T(8,128)(2,1)} %bitcast.755), channel_id=1, source_target_pairs={{0,8},{8,0},{16,24},{24,16},{1,9},{9,1},{17,25},{25,17},{2,10},{10... | collective-permute-start | bytes 7077896 | tf_op jit(solution)/shard_map/ppermute | solution.py:197
  633.4 19.7 %collective-permute-start.77 = (bf16[2,2,2,64,768]{4,3,2,1,0:T(8,128)(2,1)S(1)}, bf16[2,2,2,64,768]{4,3,2,1,0:T(8,128)(2,1)S(1)}, u32[]{:S(2)}, u32[]{:S(2)}) collective-permute-start(bf16[2,2,2,64,768]{4,3,2,1,0:T(8,128)(2,1)S(1)} %dynamic-slice_bitcast_fusion.4), channel_id=1, source_target_pairs={{0,1},{1,0},{2,3},{3,2},{4,5},{5,4},{6,7},{7,6},{8,9},{9,8},{10,11... | collective-permute-start | bytes 2359304 | tf_op jit(solution)/shard_map/ppermute | solution.py:197
  638.4 65.0 %collective-permute-start.52 = (bf16[2,2,2,2,96,768]{5,4,1,2,3,0:T(8,128)(2,1)}, bf16[2,2,2,2,96,768]{5,4,1,2,3,0:T(8,128)(2,1)}, u32[]{:S(2)}, u32[]{:S(2)}) collective-permute-start(bf16[2,2,2,2,96,768]{5,4,1,2,3,0:T(8,128)(2,1)} %bitcast.756), channel_id=1, source_target_pairs={{0,8},{8,0},{16,24},{24,16},{1,9},{9,1},{17,25},{25,17},{2,10},{10... | collective-permute-start | bytes 7077896 | tf_op jit(solution)/shard_map/ppermute | solution.py:197
  638.4 16.6 %collective-permute-start.51 = (f32[1,336]{1,0:T(1,128)S(1)}, f32[1,336]{1,0:T(1,128)S(1)}, u32[]{:S(2)}, u32[]{:S(2)}) collective-permute-start(f32[1,336]{1,0:T(1,128)S(1)} %constant_dynamic-slice_fusion.6), channel_id=1, source_target_pairs={{0,1},{1,0},{2,3},{3,2},{4,5},{5,4},{6,7},{7,6},{8,9},{9,8},{10,11... | collective-permute-start | bytes 4040 | tf_op jit(solution)/shard_map/ppermute | solution.py:197
  673.9 25.6 %collective-permute-start.61 = (bf16[2,2,2,96,768]{4,3,1,2,0:T(8,128)(2,1)}, bf16[2,2,2,96,768]{4,3,1,2,0:T(8,128)(2,1)}, u32[]{:S(2)}, u32[]{:S(2)}) collective-permute-start(bf16[2,2,2,96,768]{4,3,1,2,0:T(8,128)(2,1)} %dynamic-slice_bitcast_fusion.2), channel_id=1, source_target_pairs={{0,1},{1,0},{2,3},{3,2},{4,5},{5,4},{6,7},{7,6},{8,9},{9,8},{10,11... | collective-permute-start | bytes 3538952 | tf_op jit(solution)/shard_map/ppermute | solution.py:197
  681.1 37.5 %collective-permute-start.83 = (bf16[64,768]{1,0:T(8,128)(2,1)S(1)}, bf16[64,768]{1,0:T(8,128)(2,1)S(1)}, u32[]{:S(2)}, u32[]{:S(2)}) collective-permute-start(bf16[64,768]{1,0:T(8,128)(2,1)S(1)} %collective-permute-done.81), channel_id=1, source_target_pairs={{0,8},{8,0},{16,24},{24,16},{1,9},{9,1},{17,25},{25,17},{2,10},{10... | collective-permute-start | bytes 294920 | tf_op jit(solution)/shard_map/ppermute | solution.py:197
  701.1 16.3 %collective-permute-start.62 = (bf16[2,2,96,768]{3,2,0,1:T(8,128)(2,1)S(1)}, bf16[2,2,96,768]{3,2,0,1:T(8,128)(2,1)S(1)}, u32[]{:S(2)}, u32[]{:S(2)}) collective-permute-start(bf16[2,2,96,768]{3,2,0,1:T(8,128)(2,1)S(1)} %dynamic-slice_bitcast_fusion.6), channel_id=1, source_target_pairs={{0,16},{8,24},{16,0},{24,8},{1,17},{9,25},{17,1},{25,9},{2,18},{10... | collective-permute-start | bytes 1769480 | tf_op jit(solution)/shard_map/ppermute | solution.py:197
  701.8 72.1 %collective-permute-start.69 = (bf16[2,2,2,96,1024]{4,3,2,1,0:T(8,128)(2,1)S(1)}, bf16[2,2,2,96,1024]{4,3,2,1,0:T(8,128)(2,1)S(1)}, u32[]{:S(2)}, u32[]{:S(2)}) collective-permute-start(bf16[2,2,2,96,1024]{4,3,2,1,0:T(8,128)(2,1)S(1)} %dynamic-slice_bitcast_fusion.1), channel_id=1, source_target_pairs={{0,16},{8,24},{16,0},{24,8},{1,17},{9,25},{17,1},{25,9},{2,18},{10... | collective-permute-start | bytes 4718600 | tf_op jit(solution)/shard_map/ppermute | solution.py:197
  705.9 67.0 %collective-permute-start.53 = (bf16[2,2,2,96,768]{4,3,0,1,2:T(8,128)(2,1)S(1)}, bf16[2,2,2,96,768]{4,3,0,1,2:T(8,128)(2,1)S(1)}, u32[]{:S(2)}, u32[]{:S(2)}) collective-permute-start(bf16[2,2,2,96,768]{4,3,0,1,2:T(8,128)(2,1)S(1)} %dynamic-slice_bitcast_fusion.3), channel_id=1, source_target_pairs={{0,16},{8,24},{16,0},{24,8},{1,17},{9,25},{17,1},{25,9},{2,18},{10... | collective-permute-start | bytes 3538952 | tf_op jit(solution)/shard_map/ppermute | solution.py:197
  724.6 48.7 %collective-permute-start.64 = (bf16[96,768]{1,0:T(8,128)(2,1)S(1)}, bf16[96,768]{1,0:T(8,128)(2,1)S(1)}, u32[]{:S(2)}, u32[]{:S(2)}) collective-permute-start(bf16[96,768]{1,0:T(8,128)(2,1)S(1)} %dynamic-slice_bitcast_fusion.18), channel_id=1, source_target_pairs={{0,4},{1,5},{2,6},{3,7},{4,0},{5,1},{6,2},{7,3},{8,12},{9,13},{10,... | collective-permute-start | bytes 442376 | tf_op jit(solution)/shard_map/ppermute | solution.py:197
  773.2 16.3 %collective-permute-start.54 = (bf16[2,2,96,768]{3,2,0,1:T(8,128)(2,1)S(1)}, bf16[2,2,96,768]{3,2,0,1:T(8,128)(2,1)S(1)}, u32[]{:S(2)}, u32[]{:S(2)}) collective-permute-start(bf16[2,2,96,768]{3,2,0,1:T(8,128)(2,1)S(1)} %dynamic-slice_bitcast_fusion.7), channel_id=1, source_target_pairs={{0,1},{1,0},{2,3},{3,2},{4,5},{5,4},{6,7},{7,6},{8,9},{9,8},{10,11... | collective-permute-start | bytes 1769480 | tf_op jit(solution)/shard_map/ppermute | solution.py:197
  774.8 25.3 %collective-permute-start.70 = (bf16[2,2,96,1024]{3,2,1,0:T(8,128)(2,1)S(1)}, bf16[2,2,96,1024]{3,2,1,0:T(8,128)(2,1)S(1)}, u32[]{:S(2)}, u32[]{:S(2)}) collective-permute-start(bf16[2,2,96,1024]{3,2,1,0:T(8,128)(2,1)S(1)} %dynamic-slice_bitcast_fusion.5), channel_id=1, source_target_pairs={{0,1},{1,0},{2,3},{3,2},{4,5},{5,4},{6,7},{7,6},{8,9},{9,8},{10,11... | collective-permute-start | bytes 2359304 | tf_op jit(solution)/shard_map/ppermute | solution.py:197
  (175 other events, 1493.5 us)
